TPU v7x, 256 devices: a whole 4x4x8 slice. The times are simulated.
256 devices in a mesh: row: 64 (over z, x, core), col: 4 (over y).
Axes of the slice: x: 4, y: 4, z: 8, core: 2. Of those that a mesh axis runs over, the one named last changes fastest.
Arguments:
- features: bfloat16 [16384, 1024], P('row', 'col'), may hold values from -6 to 6
- masks: int32 [16384, 4, 1024], P('row', None, 'col'), may hold values 0 or 1
- adj_values: bfloat16 [512, 128, 128], P('row'), may hold values from 0.049804688 to 1
- adj_rows: int32 [512], P('row'), may hold values from 0 to 1, as said below
- adj_cols: int32 [512], P('row'), may hold values from 0 to 127, as said below
- adj_count: int32 [64], P('row'), may hold values from 6 to 8, as said below
- w_self_one: bfloat16 [1024, 1024], P('col'), may hold values from -0.1875 to 0.1875
- w_neigh_one: bfloat16 [1024, 1024], P('col'), may hold values from -0.1875 to 0.1875
- w_self_two: bfloat16 [1024, 1024], P('col'), may hold values from -0.1875 to 0.1875
- w_neigh_two: bfloat16 [1024, 1024], P('col'), may hold values from -0.1875 to 0.1875
Outputs:
- embeddings: bfloat16 [16384, 4, 1024], P('row', None, 'col')
Inputs may be any that keep to these rules, and one draw needn't show every extreme that they name: `adj_rows`: slot k < 2 of each device has row block k and is that device's own diagonal block; the other slots' row blocks are any of the device's 2 blocks. `adj_cols`: A slot of device r names a column block of device r - 2, r - 1, r, r + 1 or r + 2 along row. `adj_count`: some device has all 8 slots live.
All inputs are finite; a program needn't handle non-finite values. No bound on the sum of `masks` on one device may be relied on, other than what follows from the above.
Results may differ from a plain program's by a relative error of at most 0.017.
Values may be sent and summed in bfloat16 or wider, within the bound.
A program may use at most 64 MiB of HBM per device.

v0:
```python
import jax
import jax.numpy as jnp
from jax import lax
from jax.sharding import PartitionSpec as P

BS = 128


def passed_along(shard, axis, by):
    peers = lax.axis_size(axis)
    pairs = [(i, i + by) for i in range(peers) if 0 <= i + by < peers]
    return lax.ppermute(shard, axis, pairs)


def gather_rim(node_data):
    pieces = []
    for distance in (2, 1, 0, -1, -2):
        if distance == 0:
            pieces.append(node_data)
        else:
            pieces.append(passed_along(node_data, "row", distance))
    return jnp.concatenate(pieces, axis=0)


def project(inputs, agg, w_self, w_neigh):
    term = jnp.einsum("rpk,kh->rph", inputs, w_self, preferred_element_type=jnp.float32)
    term = term + jnp.einsum("rpk,kh->rph", agg, w_neigh, preferred_element_type=jnp.float32)
    return lax.psum_scatter(
        term.astype(jnp.bfloat16), "col", scatter_dimension=2, tiled=True
    ).astype(jnp.float32)


def on_device(
    features,
    masks,
    adj_values,
    adj_rows,
    adj_cols,
    adj_count,
    w_self_one,
    w_neigh_one,
    w_self_two,
    w_neigh_two,
):
    node_rows, width = features.shape
    blocks = node_rows // BS
    slots = adj_rows.shape[0]
    passes = masks.shape[1]
    me = lax.axis_index("row")
    live = jnp.arange(slots, dtype=jnp.int32) < adj_count[0]
    local = adj_cols - (me * blocks - 2 * blocks)
    placing = (
        (adj_rows[None, :] == jnp.arange(blocks, dtype=jnp.int32)[:, None]) & live[None, :]
    ).astype(jnp.float32)
    degree = jnp.dot(
        placing, jnp.sum(adj_values.astype(jnp.float32), axis=2), precision=lax.Precision.HIGHEST
    )
    scaling = lax.rsqrt(degree).reshape(node_rows, 1)
    live_values = jnp.where(live[:, None, None], adj_values, jnp.zeros_like(adj_values))

    def aggregate(extended):
        columns = extended.shape[1]
        tiles = jnp.take(extended.reshape(5 * blocks, BS, columns), local, axis=0)
        prods = jnp.einsum("sij,sjc->sic", live_values, tiles, preferred_element_type=jnp.float32)
        summed = jnp.einsum("bs,sic->bic", placing, prods, precision=lax.Precision.HIGHEST)
        return (summed.reshape(node_rows, columns) * scaling).astype(jnp.bfloat16)

    first_agg = aggregate(gather_rim(features))
    hidden = jax.nn.relu(
        project(features[:, None, :], first_agg[:, None, :], w_self_one, w_neigh_one)
    )[:, 0].astype(jnp.bfloat16)
    dropped = hidden[:, None, :] * (2 * masks).astype(jnp.bfloat16)
    outputs = []
    for pass_index in range(passes):
        single = dropped[:, pass_index]
        single_agg = aggregate(gather_rim(single))
        outputs.append(project(single[:, None, :], single_agg[:, None, :], w_self_two, w_neigh_two))
    result = jnp.concatenate(outputs, axis=1)
    return result.astype(jnp.bfloat16)


def solution(mesh):
    in_specs = (
        P("row", "col"),
        P("row", None, "col"),
        P("row", None, None),
        P("row"),
        P("row"),
        P("row"),
        P("col", None),
        P("col", None),
        P("col", None),
        P("col", None),
    )
    out_specs = P("row", None, "col")
    return jax.shard_map(
        on_device, mesh=mesh, in_specs=in_specs, out_specs=out_specs, check_vma=False
    )
```

profile of v0, /device:TPU:103, one launch (start us, length us, event | category | flops | bytes accessed | tf_op | source)
XLA Modules:
  0.0 242.1 jit_solution(2199167263000248473)
XLA Ops:
  6.5 4.8 %collective-permute-start = (bf16[256,256]{1,0:T(8,128)(2,1)}, bf16[256,256]{1,0:T(8,128)(2,1)S(1)}, u32[]{:S(2)}, u32[]{:S(2)}) collective-permute-start(bf16[256,256]{1,0:T(8,128)(2,1)} %param.12), channel_id=1, source_target_pairs={{0,8},{4,12},{8,16},{12,20},{16,24},{20,28},{24,32},{28,36},{32,40... | collective-permute-start | bytes 393224 | tf_op jit(solution)/shard_map/ppermute | solution.py:12
  11.3 4.0 %collective-permute-start.1 = (bf16[256,256]{1,0:T(8,128)(2,1)}, bf16[256,256]{1,0:T(8,128)(2,1)S(1)}, u32[]{:S(2)}, u32[]{:S(2)}) collective-permute-start(bf16[256,256]{1,0:T(8,128)(2,1)} %param.12), channel_id=1, source_target_pairs={{0,4},{4,8},{8,12},{12,16},{16,20},{20,24},{24,28},{28,32},{32,36}... | collective-permute-start | bytes 393224 | tf_op jit(solution)/shard_map/ppermute | solution.py:12
  17.2 2.2 collective-permute-start.3
  25.1 2.0 collective-permute-done.3
  31.9 22.2 %reduce-scatter.6.cloned.1.call-done = bf16[256,1,256]{2,0,1:T(8,128)(2,1)} async-done(((bf16[256,1,1024]{2,0,1:T(8,128)(2,1)}), bf16[256,1,256]{2,0,1:T(8,128)(2,1)}) %reduce-scatter.6.cloned.1.call-update) | async-done | bytes 131088 | tf_op jit(solution)/shard_map/reduce_scatter | solution.py:28
  56.1 4.4 %collective-permute-start.8 = (bf16[256,256]{1,0:T(8,128)(2,1)}, bf16[256,256]{1,0:T(8,128)(2,1)S(1)}, u32[]{:S(2)}, u32[]{:S(2)}) collective-permute-start(bf16[256,256]{1,0:T(8,128)(2,1)} %get-tuple-element.15), channel_id=1, source_target_pairs={{0,8},{4,12},{8,16},{12,20},{16,24},{20,28},{24,32},{28,36},{32,40... | collective-permute-start | bytes 393224 | tf_op jit(solution)/shard_map/ppermute | solution.py:12
  60.4 5.6 %collective-permute-start.9 = (bf16[256,256]{1,0:T(8,128)(2,1)}, bf16[256,256]{1,0:T(8,128)(2,1)S(1)}, u32[]{:S(2)}, u32[]{:S(2)}) collective-permute-start(bf16[256,256]{1,0:T(8,128)(2,1)} %get-tuple-element.15), channel_id=1, source_target_pairs={{0,4},{4,8},{8,12},{12,16},{16,20},{20,24},{24,28},{28,32},{32,36}... | collective-permute-start | bytes 393224 | tf_op jit(solution)/shard_map/ppermute | solution.py:12
  66.0 3.1 %collective-permute-start.12 = (bf16[256,256]{1,0:T(8,128)(2,1)}, bf16[256,256]{1,0:T(8,128)(2,1)S(1)}, u32[]{:S(2)}, u32[]{:S(2)}) collective-permute-start(bf16[256,256]{1,0:T(8,128)(2,1)} %get-tuple-element.14), channel_id=1, source_target_pairs={{0,8},{4,12},{8,16},{12,20},{16,24},{20,28},{24,32},{28,36},{32,40... | collective-permute-start | bytes 393224 | tf_op jit(solution)/shard_map/ppermute | solution.py:12
  69.1 2.2 collective-permute-start.13
  71.3 2.8 %collective-permute-start.16 = (bf16[256,256]{1,0:T(8,128)(2,1)S(1)}, bf16[256,256]{1,0:T(8,128)(2,1)S(1)}, u32[]{:S(2)}, u32[]{:S(2)}) collective-permute-start(bf16[256,256]{1,0:T(8,128)(2,1)S(1)} %get-tuple-element.13), channel_id=1, source_target_pairs={{0,8},{4,12},{8,16},{12,20},{16,24},{20,28},{24,32},{28,36},{32,40... | collective-permute-start | bytes 393224 | tf_op jit(solution)/shard_map/ppermute | solution.py:12
  74.5 2.7 %collective-permute-start.17 = (bf16[256,256]{1,0:T(8,128)(2,1)S(1)}, bf16[256,256]{1,0:T(8,128)(2,1)S(1)}, u32[]{:S(2)}, u32[]{:S(2)}) collective-permute-start(bf16[256,256]{1,0:T(8,128)(2,1)S(1)} %get-tuple-element.13), channel_id=1, source_target_pairs={{0,4},{4,8},{8,12},{12,16},{16,20},{20,24},{24,28},{28,32},{32,36}... | collective-permute-start | bytes 393224 | tf_op jit(solution)/shard_map/ppermute | solution.py:12
  77.2 3.1 %collective-permute-start.4 = (bf16[256,256]{1,0:T(8,128)(2,1)}, bf16[256,256]{1,0:T(8,128)(2,1)S(1)}, u32[]{:S(2)}, u32[]{:S(2)}) collective-permute-start(bf16[256,256]{1,0:T(8,128)(2,1)} %get-tuple-element.12), channel_id=1, source_target_pairs={{0,8},{4,12},{8,16},{12,20},{16,24},{20,28},{24,32},{28,36},{32,40... | collective-permute-start | bytes 393224 | tf_op jit(solution)/shard_map/ppermute | solution.py:12
  80.3 4.8 %collective-permute-start.5 = (bf16[256,256]{1,0:T(8,128)(2,1)}, bf16[256,256]{1,0:T(8,128)(2,1)S(1)}, u32[]{:S(2)}, u32[]{:S(2)}) collective-permute-start(bf16[256,256]{1,0:T(8,128)(2,1)} %get-tuple-element.12), channel_id=1, source_target_pairs={{0,4},{4,8},{8,12},{12,16},{16,20},{20,24},{24,28},{28,32},{32,36}... | collective-permute-start | bytes 393224 | tf_op jit(solution)/shard_map/ppermute | solution.py:12
  85.2 2.1 collective-permute-start.18
  87.3 2.2 collective-permute-start.19
  89.5 2.5 %collective-permute-start.14 = (bf16[256,256]{1,0:T(8,128)(2,1)}, bf16[256,256]{1,0:T(8,128)(2,1)}, u32[]{:S(2)}, u32[]{:S(2)}) collective-permute-start(bf16[256,256]{1,0:T(8,128)(2,1)} %get-tuple-element.14), channel_id=1, source_target_pairs={{4,0},{8,4},{12,8},{16,12},{20,16},{24,20},{28,24},{32,28},{36,32}... | collective-permute-start | bytes 393224 | tf_op jit(solution)/shard_map/ppermute | solution.py:12
  92.1 4.3 %collective-permute-start.15 = (bf16[256,256]{1,0:T(8,128)(2,1)}, bf16[256,256]{1,0:T(8,128)(2,1)}, u32[]{:S(2)}, u32[]{:S(2)}) collective-permute-start(bf16[256,256]{1,0:T(8,128)(2,1)} %get-tuple-element.14), channel_id=1, source_target_pairs={{8,0},{12,4},{16,8},{20,12},{24,16},{28,20},{32,24},{36,28},{40,32... | collective-permute-start | bytes 393224 | tf_op jit(solution)/shard_map/ppermute | solution.py:12
  96.4 2.2 collective-permute-start.10
  100.7 2.0 collective-permute-start.6
  104.9 2.0 collective-permute-start.7
  134.3 20.4 %reduce-scatter.8.cloned.1.call-done = bf16[256,1,256]{2,0,1:T(8,128)(2,1)} async-done(((bf16[256,1,1024]{2,0,1:T(8,128)(2,1)}), bf16[256,1,256]{2,0,1:T(8,128)(2,1)}) %reduce-scatter.8.cloned.1.call-update) | async-done | bytes 131088 | tf_op jit(solution)/shard_map/reduce_scatter | solution.py:28
  154.7 26.3 %reduce-scatter.10.cloned.1.call-done = bf16[256,1,256]{2,0,1:T(8,128)(2,1)} async-done(((bf16[256,1,1024]{2,0,1:T(8,128)(2,1)}), bf16[256,1,256]{2,0,1:T(8,128)(2,1)}) %reduce-scatter.10.cloned.1.call-update) | async-done | bytes 131088 | tf_op jit(solution)/shard_map/reduce_scatter | solution.py:28
  181.0 26.1 %reduce-scatter.12.cloned.1.call-done = bf16[256,1,256]{2,0,1:T(8,128)(2,1)} async-done(((bf16[256,1,1024]{2,0,1:T(8,128)(2,1)}), bf16[256,1,256]{2,0,1:T(8,128)(2,1)}) %reduce-scatter.12.cloned.1.call-update) | async-done | bytes 131088 | tf_op jit(solution)/shard_map/reduce_scatter | solution.py:28
  207.1 26.1 %reduce-scatter.14.cloned.1.call-done = bf16[256,1,256]{2,0,1:T(8,128)(2,1)} async-done(((bf16[256,1,1024]{2,0,1:T(8,128)(2,1)}), bf16[256,1,256]{2,0,1:T(8,128)(2,1)}) %reduce-scatter.14.cloned.1.call-update) | async-done | bytes 131088 | tf_op jit(solution)/shard_map/reduce_scatter | solution.py:28
  (126 shorter events, 47.5 us)
Async XLA Ops:
  6.5 47.6 %reduce-scatter.6.cloned.1.call-start = ((), (), s32[]{:S(2)}) async-start(), calls=%async_computation.5 | async-start | bytes 655360 | tf_op jit(solution)/shard_map/reduce_scatter | solution.py:28
  6.5 17.5 %collective-permute-start = (bf16[256,256]{1,0:T(8,128)(2,1)}, bf16[256,256]{1,0:T(8,128)(2,1)S(1)}, u32[]{:S(2)}, u32[]{:S(2)}) collective-permute-start(bf16[256,256]{1,0:T(8,128)(2,1)} %param.12), channel_id=1, source_target_pairs={{0,8},{4,12},{8,16},{12,20},{16,24},{20,28},{24,32},{28,36},{32,40... | collective-permute-start | bytes 393224 | tf_op jit(solution)/shard_map/ppermute | solution.py:12
  11.3 12.7 %collective-permute-start.1 = (bf16[256,256]{1,0:T(8,128)(2,1)}, bf16[256,256]{1,0:T(8,128)(2,1)S(1)}, u32[]{:S(2)}, u32[]{:S(2)}) collective-permute-start(bf16[256,256]{1,0:T(8,128)(2,1)} %param.12), channel_id=1, source_target_pairs={{0,4},{4,8},{8,12},{12,16},{16,20},{20,24},{24,28},{28,32},{32,36}... | collective-permute-start | bytes 393224 | tf_op jit(solution)/shard_map/ppermute | solution.py:12
  15.3 9.8 %collective-permute-start.2 = (bf16[256,256]{1,0:T(8,128)(2,1)}, bf16[256,256]{1,0:T(8,128)(2,1)S(1)}, u32[]{:S(2)}, u32[]{:S(2)}) collective-permute-start(bf16[256,256]{1,0:T(8,128)(2,1)} %param.12), channel_id=1, source_target_pairs={{4,0},{8,4},{12,8},{16,12},{20,16},{24,20},{28,24},{32,28},{36,32}... | collective-permute-start | bytes 393224 | tf_op jit(solution)/shard_map/ppermute | solution.py:12
  17.2 9.9 %collective-permute-start.3 = (bf16[256,256]{1,0:T(8,128)(2,1)}, bf16[256,256]{1,0:T(8,128)(2,1)S(1)}, u32[]{:S(2)}, u32[]{:S(2)}) collective-permute-start(bf16[256,256]{1,0:T(8,128)(2,1)} %param.12), channel_id=1, source_target_pairs={{8,0},{12,4},{16,8},{20,12},{24,16},{28,20},{32,24},{36,28},{40,32... | collective-permute-start | bytes 393224 | tf_op jit(solution)/shard_map/ppermute | solution.py:12
  31.9 122.8 %reduce-scatter.8.cloned.1.call-start = ((), (), s32[]{:S(2)}) async-start(), calls=%async_computation.6 | async-start | bytes 655360 | tf_op jit(solution)/shard_map/reduce_scatter | solution.py:28
  56.1 18.4 %collective-permute-start.8 = (bf16[256,256]{1,0:T(8,128)(2,1)}, bf16[256,256]{1,0:T(8,128)(2,1)S(1)}, u32[]{:S(2)}, u32[]{:S(2)}) collective-permute-start(bf16[256,256]{1,0:T(8,128)(2,1)} %get-tuple-element.15), channel_id=1, source_target_pairs={{0,8},{4,12},{8,16},{12,20},{16,24},{20,28},{24,32},{28,36},{32,40... | collective-permute-start | bytes 393224 | tf_op jit(solution)/shard_map/ppermute | solution.py:12
  60.4 26.9 %collective-permute-start.9 = (bf16[256,256]{1,0:T(8,128)(2,1)}, bf16[256,256]{1,0:T(8,128)(2,1)S(1)}, u32[]{:S(2)}, u32[]{:S(2)}) collective-permute-start(bf16[256,256]{1,0:T(8,128)(2,1)} %get-tuple-element.15), channel_id=1, source_target_pairs={{0,4},{4,8},{8,12},{12,16},{16,20},{20,24},{24,28},{28,32},{32,36}... | collective-permute-start | bytes 393224 | tf_op jit(solution)/shard_map/ppermute | solution.py:12
  66.0 11.1 %collective-permute-start.12 = (bf16[256,256]{1,0:T(8,128)(2,1)}, bf16[256,256]{1,0:T(8,128)(2,1)S(1)}, u32[]{:S(2)}, u32[]{:S(2)}) collective-permute-start(bf16[256,256]{1,0:T(8,128)(2,1)} %get-tuple-element.14), channel_id=1, source_target_pairs={{0,8},{4,12},{8,16},{12,20},{16,24},{20,28},{24,32},{28,36},{32,40... | collective-permute-start | bytes 393224 | tf_op jit(solution)/shard_map/ppermute | solution.py:12
  69.1 20.4 %collective-permute-start.13 = (bf16[256,256]{1,0:T(8,128)(2,1)}, bf16[256,256]{1,0:T(8,128)(2,1)S(1)}, u32[]{:S(2)}, u32[]{:S(2)}) collective-permute-start(bf16[256,256]{1,0:T(8,128)(2,1)} %get-tuple-element.14), channel_id=1, source_target_pairs={{0,4},{4,8},{8,12},{12,16},{16,20},{20,24},{24,28},{28,32},{32,36}... | collective-permute-start | bytes 393224 | tf_op jit(solution)/shard_map/ppermute | solution.py:12
  71.3 9.0 %collective-permute-start.16 = (bf16[256,256]{1,0:T(8,128)(2,1)S(1)}, bf16[256,256]{1,0:T(8,128)(2,1)S(1)}, u32[]{:S(2)}, u32[]{:S(2)}) collective-permute-start(bf16[256,256]{1,0:T(8,128)(2,1)S(1)} %get-tuple-element.13), channel_id=1, source_target_pairs={{0,8},{4,12},{8,16},{12,20},{16,24},{20,28},{24,32},{28,36},{32,40... | collective-permute-start | bytes 393224 | tf_op jit(solution)/shard_map/ppermute | solution.py:12
  74.5 17.6 %collective-permute-start.17 = (bf16[256,256]{1,0:T(8,128)(2,1)S(1)}, bf16[256,256]{1,0:T(8,128)(2,1)S(1)}, u32[]{:S(2)}, u32[]{:S(2)}) collective-permute-start(bf16[256,256]{1,0:T(8,128)(2,1)S(1)} %get-tuple-element.13), channel_id=1, source_target_pairs={{0,4},{4,8},{8,12},{12,16},{16,20},{20,24},{24,28},{28,32},{32,36}... | collective-permute-start | bytes 393224 | tf_op jit(solution)/shard_map/ppermute | solution.py:12
  80.3 16.1 %collective-permute-start.5 = (bf16[256,256]{1,0:T(8,128)(2,1)}, bf16[256,256]{1,0:T(8,128)(2,1)S(1)}, u32[]{:S(2)}, u32[]{:S(2)}) collective-permute-start(bf16[256,256]{1,0:T(8,128)(2,1)} %get-tuple-element.12), channel_id=1, source_target_pairs={{0,4},{4,8},{8,12},{12,16},{16,20},{20,24},{24,28},{28,32},{32,36}... | collective-permute-start | bytes 393224 | tf_op jit(solution)/shard_map/ppermute | solution.py:12
  85.2 13.5 %collective-permute-start.18 = (bf16[256,256]{1,0:T(8,128)(2,1)S(1)}, bf16[256,256]{1,0:T(8,128)(2,1)S(1)}, u32[]{:S(2)}, u32[]{:S(2)}) collective-permute-start(bf16[256,256]{1,0:T(8,128)(2,1)S(1)} %get-tuple-element.13), channel_id=1, source_target_pairs={{4,0},{8,4},{12,8},{16,12},{20,16},{24,20},{28,24},{32,28},{36,32}... | collective-permute-start | bytes 393224 | tf_op jit(solution)/shard_map/ppermute | solution.py:12
  87.3 13.3 %collective-permute-start.19 = (bf16[256,256]{1,0:T(8,128)(2,1)S(1)}, bf16[256,256]{1,0:T(8,128)(2,1)S(1)}, u32[]{:S(2)}, u32[]{:S(2)}) collective-permute-start(bf16[256,256]{1,0:T(8,128)(2,1)S(1)} %get-tuple-element.13), channel_id=1, source_target_pairs={{8,0},{12,4},{16,8},{20,12},{24,16},{28,20},{32,24},{36,28},{40,32... | collective-permute-start | bytes 393224 | tf_op jit(solution)/shard_map/ppermute | solution.py:12
  89.5 15.4 %collective-permute-start.14 = (bf16[256,256]{1,0:T(8,128)(2,1)}, bf16[256,256]{1,0:T(8,128)(2,1)}, u32[]{:S(2)}, u32[]{:S(2)}) collective-permute-start(bf16[256,256]{1,0:T(8,128)(2,1)} %get-tuple-element.14), channel_id=1, source_target_pairs={{4,0},{8,4},{12,8},{16,12},{20,16},{24,20},{28,24},{32,28},{36,32}... | collective-permute-start | bytes 393224 | tf_op jit(solution)/shard_map/ppermute | solution.py:12
  92.1 16.4 %collective-permute-start.15 = (bf16[256,256]{1,0:T(8,128)(2,1)}, bf16[256,256]{1,0:T(8,128)(2,1)}, u32[]{:S(2)}, u32[]{:S(2)}) collective-permute-start(bf16[256,256]{1,0:T(8,128)(2,1)} %get-tuple-element.14), channel_id=1, source_target_pairs={{8,0},{12,4},{16,8},{20,12},{24,16},{28,20},{32,24},{36,28},{40,32... | collective-permute-start | bytes 393224 | tf_op jit(solution)/shard_map/ppermute | solution.py:12
  96.4 16.9 %collective-permute-start.10 = (bf16[256,256]{1,0:T(8,128)(2,1)}, bf16[256,256]{1,0:T(8,128)(2,1)}, u32[]{:S(2)}, u32[]{:S(2)}) collective-permute-start(bf16[256,256]{1,0:T(8,128)(2,1)} %get-tuple-element.15), channel_id=1, source_target_pairs={{4,0},{8,4},{12,8},{16,12},{20,16},{24,20},{28,24},{32,28},{36,32}... | collective-permute-start | bytes 393224 | tf_op jit(solution)/shard_map/ppermute | solution.py:12
  98.7 16.1 %collective-permute-start.11 = (bf16[256,256]{1,0:T(8,128)(2,1)}, bf16[256,256]{1,0:T(8,128)(2,1)}, u32[]{:S(2)}, u32[]{:S(2)}) collective-permute-start(bf16[256,256]{1,0:T(8,128)(2,1)} %get-tuple-element.15), channel_id=1, source_target_pairs={{8,0},{12,4},{16,8},{20,12},{24,16},{28,20},{32,24},{36,28},{40,32... | collective-permute-start | bytes 393224 | tf_op jit(solution)/shard_map/ppermute | solution.py:12
  100.7 20.4 %collective-permute-start.6 = (bf16[256,256]{1,0:T(8,128)(2,1)}, bf16[256,256]{1,0:T(8,128)(2,1)}, u32[]{:S(2)}, u32[]{:S(2)}) collective-permute-start(bf16[256,256]{1,0:T(8,128)(2,1)} %get-tuple-element.12), channel_id=1, source_target_pairs={{4,0},{8,4},{12,8},{16,12},{20,16},{24,20},{28,24},{32,28},{36,32}... | collective-permute-start | bytes 393224 | tf_op jit(solution)/shard_map/ppermute | solution.py:12
  104.9 17.8 %collective-permute-start.7 = (bf16[256,256]{1,0:T(8,128)(2,1)}, bf16[256,256]{1,0:T(8,128)(2,1)S(1)}, u32[]{:S(2)}, u32[]{:S(2)}) collective-permute-start(bf16[256,256]{1,0:T(8,128)(2,1)} %get-tuple-element.12), channel_id=1, source_target_pairs={{8,0},{12,4},{16,8},{20,12},{24,16},{28,20},{32,24},{36,28},{40,32... | collective-permute-start | bytes 393224 | tf_op jit(solution)/shard_map/ppermute | solution.py:12
  129.8 51.2 %reduce-scatter.10.cloned.1.call-start = ((), (), s32[]{:S(2)}) async-start(), calls=%async_computation.7 | async-start | bytes 655360 | tf_op jit(solution)/shard_map/reduce_scatter | solution.py:28
  131.3 75.8 %reduce-scatter.12.cloned.1.call-start = ((), (), s32[]{:S(2)}) async-start(), calls=%async_computation.8 | async-start | bytes 655360 | tf_op jit(solution)/shard_map/reduce_scatter | solution.py:28
  132.8 100.5 %reduce-scatter.14.cloned.1.call-start = ((), (), s32[]{:S(2)}) async-start(), calls=%async_computation.9 | async-start | bytes 655360 | tf_op jit(solution)/shard_map/reduce_scatter | solution.py:28
  (16 other events, 126.5 us)
Sparse Core Ops, SparseCore 0:
  32.0 22.0 reduce-scatter.5
  129.9 24.7 reduce-scatter.7
  157.2 23.7 reduce-scatter.9
  183.4 23.7 reduce-scatter.11
  209.5 23.7 reduce-scatter.13
where the time goes:
time: 246 us; the launch traced here: 242 us
  waiting for transfers between devices  124 us (50%)
  starting transfers between devices  60.9 us (25%)
  local copies, waits for them, and re-layouts  22.8 us (9%)
  matrix products  15.8 us (6%)
  between operations  14.6 us (6%)
  other arithmetic  3.71 us (2%)
    reduce_scatter x5, waiting for transfers between devices, project(): lax.psum_scatter(term.astype(jnp.bfloat16), 'col', scatter_dimension=2, t...  121 us
    ppermute x20, starting transfers between devices, passed_along(): return lax.ppermute(shard, axis, pairs)  60.7 us
    unnamed x47, local copies, waits for them, and re-layouts  9.34 us
    gather x5, local copies, waits for them, and re-layouts, aggregate(): tiles = jnp.take(extended.reshape(5 * blocks, BS, columns), local, axis=0)  6.16 us
    dot_general x5, matrix products, aggregate(): jnp.einsum('bs,sic->bic', placing, prods, precision=lax.Precision.HIGHEST)  5.83 us
    dot_general x5, matrix products, project(): jnp.einsum('rpk,kh->rph', agg, w_neigh, preferred_element_type=jnp.float32)  5.51 us
  transfers between devices with their start and end apart: 25, of which 7 were waited for; matrix products, arithmetic and copies ran while one was open for 10% of the time, Pallas kernels for 0%

commit v1 on v0

v1 whole, which is shorter than its diff:
```python
import functools

import jax
import jax.numpy as jnp
from jax import lax
from jax.experimental import pallas as pl
from jax.experimental.pallas import tpu as pltpu
from jax.sharding import PartitionSpec as P

BS = 128
MESH = pl.DeviceIdType.MESH
ROW_OFFSETS = (2, -2, 1, -1)
COL_OFFSETS = (2, 1, 3)
BF16, F32 = jnp.bfloat16, jnp.float32


def fused(n_row, n_col, passes, blocks, slots, *refs):
    (features, masks, adj, adj_rows, adj_cols, adj_count, w_self_one, w_neigh_one,
     w_self_two, w_neigh_two, out) = refs[:11]
    rest = list(refs[11:])
    rows_s, cols_s, count_s, adj_v, placed, scale, ws1, wn1, ws2, wn2, mask_v = rest[:11]
    self_one, self_two, term_one, got_one, term_two, got_two, ext_one = rest[11:18]
    ext_two = rest[18:18 + passes]
    (load_sem, mask_sem, f_send, f_recv, d_send, d_recv, one_send, one_recv, two_send,
     two_recv) = rest[18 + passes:]

    r, c = lax.axis_index("row"), lax.axis_index("col")
    node_rows = blocks * BS

    def on_row(by):
        return (lax.rem(r + by + n_row, n_row), c)

    def on_col(by):
        return (r, lax.rem(c + by, n_col))

    barrier = pltpu.get_barrier_semaphore()
    for by in ROW_OFFSETS:
        pl.semaphore_signal(barrier, 1, device_id=on_row(by), device_id_type=MESH)
    for by in COL_OFFSETS:
        pl.semaphore_signal(barrier, 1, device_id=on_col(by), device_id_type=MESH)

    loads = []
    own = ext_one.at[pl.ds(2 * blocks, blocks)]
    for i, (src, dst) in enumerate(
        ((features, own), (adj, adj_v), (adj_rows, rows_s), (adj_cols, cols_s),
         (adj_count, count_s), (w_self_one, ws1), (w_neigh_one, wn1), (w_self_two, ws2),
         (w_neigh_two, wn2))
    ):
        loads.append(pltpu.make_async_copy(src, dst, load_sem.at[i]))
    mask_loads = [
        pltpu.make_async_copy(masks.at[:, p, :], mask_v.at[p], mask_sem.at[p])
        for p in range(passes)
    ]
    for copy in loads + mask_loads:
        copy.start()
    loads[0].wait()
    pl.semaphore_wait(barrier, len(ROW_OFFSETS) + len(COL_OFFSETS))

    def exchange(ext, send, recv):
        copies = []
        for i, by in enumerate(ROW_OFFSETS):
            copy = pltpu.make_async_remote_copy(
                src_ref=ext.at[pl.ds(2 * blocks, blocks)],
                dst_ref=ext.at[pl.ds((2 - by) * blocks, blocks)],
                send_sem=send.at[i], recv_sem=recv.at[i],
                device_id=on_row(by), device_id_type=MESH)
            copy.start()
            copies.append(copy)
        return copies

    f_copies = exchange(ext_one, f_send, f_recv)

    for copy in loads[1:5]:
        copy.wait()
    me = r * blocks - 2 * blocks
    local = [jnp.clip(cols_s[s] - me, 0, 5 * blocks - 1) for s in range(slots)]
    for s in range(slots):
        live = s < count_s[0]
        for b in range(blocks):
            here = jnp.logical_and(live, rows_s[s] == b)
            keep = jnp.where(here, 1.0, 0.0).astype(BF16)
            placed[pl.ds(b * BS, BS), pl.ds(s * BS, BS)] = adj_v[s] * keep
    degree = jnp.dot(placed[...], jnp.ones((slots * BS, 2 * BS), BF16),
                     preferred_element_type=F32)
    scale[...] = lax.rsqrt(degree)

    def aggregate(ext):
        tiles = jnp.concatenate([ext[i] for i in local], axis=0)
        summed = jnp.dot(placed[...], tiles, preferred_element_type=F32)
        return (summed * scale[...]).astype(BF16)

    width = node_rows

    def quarter(k):
        return pl.ds(pl.multiple_of(lax.rem(c + k, n_col) * width, width), width)

    def spread(agg, self_term, w_neigh, term, got, send, recv):
        copies = []
        for k in COL_OFFSETS + (0,):
            total = self_term[k] + jnp.dot(
                agg, w_neigh[:, quarter(k)], preferred_element_type=F32)
            term[k] = total.astype(BF16)
            if k:
                copy = pltpu.make_async_remote_copy(
                    src_ref=term.at[k], dst_ref=got.at[k - 1],
                    send_sem=send.at[k - 1], recv_sem=recv.at[k - 1],
                    device_id=on_col(k), device_id_type=MESH)
                copy.start()
                copies.append(copy)
        return copies

    def gathered(term, got):
        total = term[0].astype(F32)
        for k in range(1, n_col):
            total = total + got[k - 1].astype(F32)
        return total

    def self_project(own_ref, w_self, self_term):
        mine = jnp.concatenate([own_ref[2 * blocks + b] for b in range(blocks)], axis=0)
        for k in range(n_col):
            self_term[k] = jnp.dot(mine, w_self[:, quarter(k)], preferred_element_type=F32)

    loads[5].wait()
    self_project(ext_one, ws1, self_one)
    for copy in loads[6:]:
        copy.wait()
    for copy in f_copies:
        copy.wait_recv()
    one = spread(aggregate(ext_one), self_one, wn1, term_one, got_one, one_send, one_recv)
    for copy in mask_loads:
        copy.wait()
    for copy in one:
        copy.wait_recv()
    hidden = jnp.maximum(gathered(term_one, got_one), 0.0).astype(BF16)
    doubled = (hidden + hidden).astype(F32)
    d_copies = []
    for p in range(passes):
        dropped = (doubled * mask_v[p].astype(F32)).astype(BF16)
        for b in range(blocks):
            ext_two[p][2 * blocks + b] = dropped[b * BS:(b + 1) * BS]
        d_copies.append(exchange(ext_two[p], d_send.at[p], d_recv.at[p]))
    for p in range(passes):
        self_project(ext_two[p], ws2, self_two.at[p])
    two = []
    for p in range(passes):
        for copy in d_copies[p]:
            copy.wait_recv()
        two.append(spread(aggregate(ext_two[p]), self_two.at[p], wn2, term_two.at[p],
                          got_two.at[p], two_send.at[p], two_recv.at[p]))
    for p in range(passes):
        for copy in two[p]:
            copy.wait_recv()
        out[p] = gathered(term_two.at[p], got_two.at[p]).astype(BF16)
    for group in [f_copies, one] + d_copies + two:
        for copy in group:
            copy.wait_send()


def interleave(stacked, out):
    passes, rows, _ = stacked.shape
    step = 32
    for low in range(0, rows, step):
        part = stacked[:, low:low + step, :].astype(F32)
        out[low:low + step] = jnp.swapaxes(part, 0, 1).astype(BF16)


def solution(mesh):
    n_row, n_col = mesh.shape["row"], mesh.shape["col"]

    def on_device(features, masks, adj, adj_rows, adj_cols, adj_count, *weights):
        node_rows, width = features.shape
        blocks, slots, passes = node_rows // BS, adj_rows.shape[0], masks.shape[1]
        hidden = weights[0].shape[1]
        dma = pltpu.SemaphoreType.DMA
        tile = (node_rows, width)
        ext = pltpu.VMEM((5 * blocks, BS, width), BF16)
        any_spec = pl.BlockSpec(memory_space=pl.ANY)
        vmem_spec = pl.BlockSpec(memory_space=pltpu.VMEM)
        stacked = pl.pallas_call(
            functools.partial(fused, n_row, n_col, passes, blocks, slots),
            out_shape=jax.ShapeDtypeStruct((passes,) + tile, BF16),
            in_specs=[any_spec] * 10,
            out_specs=vmem_spec,
            scratch_shapes=[
                pltpu.SMEM((slots,), jnp.int32), pltpu.SMEM((slots,), jnp.int32),
                pltpu.SMEM((1,), jnp.int32),
                pltpu.VMEM(adj.shape, BF16), pltpu.VMEM((node_rows, slots * BS), BF16),
                pltpu.VMEM(tile, F32),
            ] + [pltpu.VMEM((width, hidden), BF16)] * 4 + [
                pltpu.VMEM((passes,) + tile, jnp.int32),
                pltpu.VMEM((n_col,) + tile, F32), pltpu.VMEM((passes, n_col) + tile, F32),
                pltpu.VMEM((n_col,) + tile, BF16), pltpu.VMEM((n_col - 1,) + tile, BF16),
                pltpu.VMEM((passes, n_col) + tile, BF16),
                pltpu.VMEM((passes, n_col - 1) + tile, BF16),
            ] + [ext] * (1 + passes) + [
                dma((9,)), dma((passes,)), dma((4,)), dma((4,)), dma((passes, 4)),
                dma((passes, 4)), dma((n_col - 1,)), dma((n_col - 1,)),
                dma((passes, n_col - 1)), dma((passes, n_col - 1)),
            ],
            compiler_params=pltpu.CompilerParams(
                collective_id=0, has_side_effects=True, vmem_limit_bytes=48 * 2**20),
        )(features.reshape(blocks, BS, width), masks, adj, adj_rows, adj_cols, adj_count, *weights)
        return pl.pallas_call(
            interleave,
            out_shape=jax.ShapeDtypeStruct((node_rows, passes, width), BF16),
            in_specs=[vmem_spec],
            out_specs=vmem_spec,
            compiler_params=pltpu.CompilerParams(vmem_limit_bytes=16 * 2**20),
        )(stacked)

    in_specs = (
        P("row", "col"), P("row", None, "col"), P("row", None, None), P("row"), P("row"),
        P("row"), P("col", None), P("col", None), P("col", None), P("col", None),
    )
    return jax.shard_map(on_device, mesh=mesh, in_specs=in_specs,
                         out_specs=P("row", None, "col"), check_vma=False)
```

time: 246 us -> 66.8 us (0.27)
  the two profiles are of different devices: /device:TPU:103 before, /device:TPU:8 now
where the time goes in v1:
time: 66.8 us; the launch traced here: 66.5 us
  Pallas kernels  57.9 us (87%)
  local copies, waits for them, and re-layouts  7.9 us (12%)
  between operations  0.68 us (1%)
    pallas_call x1, Pallas kernels, on_device(): pl.pallas_call(functools.partial(fused, n_row, n_col, passes, blocks, slo...  56.8 us
    unnamed x18, local copies, waits for them, and re-layouts  7.9 us

profile of v1, /device:TPU:8, one launch (start us, length us, event | category | flops | bytes accessed | tf_op | source)
XLA Modules:
  0.0 66.5 jit_solution(860934614390765773)
XLA Ops:
  0.7 0.0 copy-start.7
  0.7 0.0 copy-start.8
  0.7 0.6 copy-done.7
  1.3 0.0 copy-done.8
  1.3 0.0 copy-start
  1.3 1.2 %copy-done = s32[256,4,256]{2,1,0:T(4,128)S(1)} copy-done((s32[256,4,256]{2,1,0:T(4,128)S(1)}, s32[256,4,256]{2,1,0:T(4,128)}, u32[]{:S(2)}) %copy-start) | copy-done | bytes 1048600
  2.5 0.0 copy-start.1
  2.6 1.0 %copy-done.1 = bf16[256,1024]{1,0:T(8,128)(2,1)S(1)} copy-done((bf16[256,1024]{1,0:T(8,128)(2,1)S(1)}, bf16[256,1024]{1,0:T(8,128)(2,1)}, u32[]{:S(2)}) %copy-start.1) | copy-done | bytes 524312
  3.6 0.0 copy-start.2
  3.6 1.0 %copy-done.2 = bf16[256,1024]{1,0:T(8,128)(2,1)S(1)} copy-done((bf16[256,1024]{1,0:T(8,128)(2,1)S(1)}, bf16[256,1024]{1,0:T(8,128)(2,1)}, u32[]{:S(2)}) %copy-start.2) | copy-done | bytes 524312
  4.6 0.0 copy-start.3
  4.6 1.0 %copy-done.3 = bf16[256,1024]{1,0:T(8,128)(2,1)S(1)} copy-done((bf16[256,1024]{1,0:T(8,128)(2,1)S(1)}, bf16[256,1024]{1,0:T(8,128)(2,1)}, u32[]{:S(2)}) %copy-start.3) | copy-done | bytes 524312
  5.7 0.0 copy-start.4
  5.7 1.0 %copy-done.4 = bf16[256,1024]{1,0:T(8,128)(2,1)S(1)} copy-done((bf16[256,1024]{1,0:T(8,128)(2,1)S(1)}, bf16[256,1024]{1,0:T(8,128)(2,1)}, u32[]{:S(2)}) %copy-start.4) | copy-done | bytes 524312
  6.7 0.0 copy-start.5
  6.7 0.9 %copy-done.5 = bf16[8,128,128]{2,1,0:T(8,128)(2,1)S(1)} copy-done((bf16[8,128,128]{2,1,0:T(8,128)(2,1)S(1)}, bf16[8,128,128]{2,1,0:T(8,128)(2,1)}, u32[]{:S(2)}) %copy-start.5) | copy-done | bytes 262168
  7.7 0.0 copy-start.6
  7.7 0.9 %copy-done.6 = bf16[256,256]{1,0:T(8,128)(2,1)S(1)} copy-done((bf16[256,256]{1,0:T(8,128)(2,1)S(1)}, bf16[256,256]{1,0:T(8,128)(2,1)}, u32[]{:S(2)}) %copy-start.6) | copy-done | bytes 131096
  8.6 56.8 %shard_map.100.stacked = bf16[4,256,256]{2,1,0:T(8,128)(2,1)S(1)} custom-call(bf16[2,128,256]{2,1,0:T(8,128)(2,1)S(1)} %bitcast.1, s32[256,4,256]{2,1,0:T(4,128)S(1)} %copy-done, bf16[8,128,128]{2,1,0:T(8,128)(2,1)S(1)} %copy-done.5, s32[8]{0:T(128)S(1)} %copy-done.7, s32[8]{0:T(128)S(1)} %copy-done.8, s32[1]{0:T(128)S(6)} %copy.11.refs_5_, ...), custom_call_target="tpu_custom_call" | custom-call | tf_op jit(solution)/shard_map/pallas_call | solution.py:179
  65.4 1.1 %shard_map.101 = bf16[256,4,256]{2,1,0:T(4,128)(2,1)} custom-call(bf16[4,256,256]{2,1,0:T(8,128)(2,1)S(1)} %shard_map.100.stacked), custom_call_target="tpu_custom_call" | custom-call | tf_op jit(solution)/shard_map/pallas_call | solution.py:203
Async XLA Ops:
  0.7 0.7 copy-start.7
  0.7 0.7 copy-start.8
  1.3 1.2 %copy-start = (s32[256,4,256]{2,1,0:T(4,128)S(1)}, s32[256,4,256]{2,1,0:T(4,128)}, u32[]{:S(2)}) copy-start(s32[256,4,256]{2,1,0:T(4,128)} %refs_1_.1) | copy-start | bytes 3145732
  2.5 1.0 %copy-start.1 = (bf16[256,1024]{1,0:T(8,128)(2,1)S(1)}, bf16[256,1024]{1,0:T(8,128)(2,1)}, u32[]{:S(2)}) copy-start(bf16[256,1024]{1,0:T(8,128)(2,1)} %refs_6_.1) | copy-start | bytes 1572868
  3.6 1.0 %copy-start.2 = (bf16[256,1024]{1,0:T(8,128)(2,1)S(1)}, bf16[256,1024]{1,0:T(8,128)(2,1)}, u32[]{:S(2)}) copy-start(bf16[256,1024]{1,0:T(8,128)(2,1)} %refs_7_.1) | copy-start | bytes 1572868
  4.6 1.0 %copy-start.3 = (bf16[256,1024]{1,0:T(8,128)(2,1)S(1)}, bf16[256,1024]{1,0:T(8,128)(2,1)}, u32[]{:S(2)}) copy-start(bf16[256,1024]{1,0:T(8,128)(2,1)} %refs_8_.1) | copy-start | bytes 1572868
  5.7 1.0 %copy-start.4 = (bf16[256,1024]{1,0:T(8,128)(2,1)S(1)}, bf16[256,1024]{1,0:T(8,128)(2,1)}, u32[]{:S(2)}) copy-start(bf16[256,1024]{1,0:T(8,128)(2,1)} %refs_9_.1) | copy-start | bytes 1572868
  6.7 0.9 %copy-start.5 = (bf16[8,128,128]{2,1,0:T(8,128)(2,1)S(1)}, bf16[8,128,128]{2,1,0:T(8,128)(2,1)}, u32[]{:S(2)}) copy-start(bf16[8,128,128]{2,1,0:T(8,128)(2,1)} %refs_2_.1) | copy-start | bytes 786436
  7.7 0.9 %copy-start.6 = (bf16[256,256]{1,0:T(8,128)(2,1)S(1)}, bf16[256,256]{1,0:T(8,128)(2,1)}, u32[]{:S(2)}) copy-start(bf16[256,256]{1,0:T(8,128)(2,1)} %param.10) | copy-start | bytes 393220

commit v2 on v1

--- a/solution.py
+++ b/solution.py
@@ -178,7 +178,7 @@
         vmem_spec = pl.BlockSpec(memory_space=pltpu.VMEM)
         stacked = pl.pallas_call(
             functools.partial(fused, n_row, n_col, passes, blocks, slots),
-            out_shape=jax.ShapeDtypeStruct((passes,) + tile, BF16),
+            out_shape=pltpu.VMEM((passes,) + tile, BF16),
             in_specs=[any_spec] * 10,
             out_specs=vmem_spec,
             scratch_shapes=[
@@ -199,7 +199,8 @@
             ],
             compiler_params=pltpu.CompilerParams(
                 collective_id=0, has_side_effects=True, vmem_limit_bytes=48 * 2**20),
-        )(features.reshape(blocks, BS, width), masks, adj, adj_rows, adj_cols, adj_count, *weights)
+        )(*[pltpu.with_memory_space_constraint(x, pltpu.HBM) if x.size > 1 else x for x in (
+            features.reshape(blocks, BS, width), masks, adj, adj_rows, adj_cols, adj_count, *weights)])
         return pl.pallas_call(
             interleave,
             out_shape=jax.ShapeDtypeStruct((node_rows, passes, width), BF16),

time: 66.8 us -> 58.8 us (0.88)
  local copies, waits for them, and re-layouts: 7.9 us -> 0 us
    unnamed x18 -> x0, local copies, waits for them, and re-layouts: 7.9 us -> none
where the time goes in v2:
time: 58.8 us; the launch traced here: 58.7 us
  Pallas kernels  58 us (99%)
  between operations  0.66 us (1%)
    pallas_call x1, Pallas kernels, on_device(): pl.pallas_call(functools.partial(fused, n_row, n_col, passes, blocks, slo...  57 us

profile of v2, /device:TPU:8, one launch (start us, length us, event | category | flops | bytes accessed | tf_op | source)
XLA Modules:
  0.0 58.7 jit_solution(7060861873170013161)
XLA Ops:
  0.7 57.0 %shard_map.100.stacked = bf16[4,256,256]{2,1,0:T(8,128)(2,1)S(1)} custom-call(bf16[2,128,256]{2,1,0:T(8,128)(2,1)} %bitcast.1, s32[256,4,256]{2,1,0:T(4,128)} %refs_1_.1, bf16[8,128,128]{2,1,0:T(8,128)(2,1)} %refs_2_.1, s32[8]{0:T(128)} %refs_3_.1, s32[8]{0:T(128)} %refs_4_.1, s32[1]{0:T(128)S(6)} %copy.11.refs_5_, bf16[256,1024]{1,0:T(8,128)(2,1)} %refs_6_.1, ...), custom_call_target="tpu_custom_call" | custom-call | tf_op jit(solution)/shard_map/pallas_call | solution.py:179
  57.6 1.1 %shard_map.101 = bf16[256,4,256]{2,1,0:T(4,128)(2,1)} custom-call(bf16[4,256,256]{2,1,0:T(8,128)(2,1)S(1)} %shard_map.100.stacked), custom_call_target="tpu_custom_call" | custom-call | tf_op jit(solution)/shard_map/pallas_call | solution.py:204

commit v3 on v2

v3 whole, which is shorter than its diff:
```python
import functools

import jax
import jax.numpy as jnp
from jax import lax
from jax.experimental import pallas as pl
from jax.experimental.pallas import tpu as pltpu
from jax.sharding import PartitionSpec as P

BS = 128
MESH = pl.DeviceIdType.MESH
BF16, F32 = jnp.bfloat16, jnp.float32


def fused(n_row, n_col, passes, blocks, slots, *refs):
    (features, masks, adj, adj_rows, adj_cols, adj_count, w_self_one, w_neigh_one,
     w_self_two, w_neigh_two, out) = refs[:11]
    rest = list(refs[11:])
    rows_s, cols_s, count_s, adj_v, placed, scale, ws1, wn1, ws2, wn2, mask_v = rest[:11]
    self_term, term, mid, relayed, got = rest[11:16]
    ext = rest[16:17 + passes]
    load_sem, mask_sem, row_send, row_recv, col_send, col_recv = rest[17 + passes:]

    r, c = lax.axis_index("row"), lax.axis_index("col")
    odd = lax.rem(r, 2)
    has_left, has_right = r >= 2, r < n_row - 2
    inner = jnp.where(odd == 0, has_right, has_left)
    outer = jnp.where(odd == 0, has_left, has_right)
    sibling = (r + 1 - 2 * odd, c)
    far_right, far_left = (lax.rem(r + 2, n_row), c), (lax.rem(r + n_row - 2, n_row), c)
    col_right, col_left = (r, lax.rem(c + 1, n_col)), (r, lax.rem(c + n_col - 1, n_col))
    node_rows = blocks * BS
    half = node_rows // 2

    barrier = pltpu.get_barrier_semaphore()

    def greet(device):
        pl.semaphore_signal(barrier, 1, device_id=device, device_id_type=MESH)

    pl.when(has_right)(lambda: greet(far_right))
    pl.when(has_left)(lambda: greet(far_left))
    for device in (sibling, col_right, col_left):
        greet(device)

    loads = []
    own = ext[0].at[pl.ds(2 * blocks, blocks)]
    for i, (src, dst) in enumerate(
        ((features, own), (adj, adj_v), (adj_rows, rows_s), (adj_cols, cols_s),
         (adj_count, count_s), (w_self_one, ws1), (w_neigh_one, wn1), (w_self_two, ws2),
         (w_neigh_two, wn2))
    ):
        loads.append(pltpu.make_async_copy(src, dst, load_sem.at[i]))
    mask_loads = [
        pltpu.make_async_copy(masks.at[:, p, :], mask_v.at[p], mask_sem.at[p])
        for p in range(passes)
    ]
    for copy in loads + mask_loads:
        copy.start()
    loads[0].wait()
    pl.semaphore_wait(barrier, 3 + has_left.astype(jnp.int32) + has_right.astype(jnp.int32))

    def remote(src, dst, send, recv, device):
        return pltpu.make_async_remote_copy(
            src_ref=src, dst_ref=dst, send_sem=send, recv_sem=recv, device_id=device,
            device_id_type=MESH)

    def row_copy(stage, i):
        src, dst, device = (
            (2, 0, far_right), (2, 4, far_left), (2, 1 + 2 * odd, sibling),
            (4 - 4 * odd, 3 - 2 * odd, sibling))[i]
        pairs = [ext[stage].at[pl.ds(n * blocks, blocks)] for n in (src, dst)]
        return remote(*pairs, row_send.at[stage, i], row_recv.at[stage, i], device)

    def row_start(stage):
        pl.when(has_right)(lambda: row_copy(stage, 0).start())
        pl.when(has_left)(lambda: row_copy(stage, 1).start())
        row_copy(stage, 2).start()

    def row_wait(stage):
        pl.when(has_left)(lambda: row_copy(stage, 0).wait_recv())
        pl.when(has_right)(lambda: row_copy(stage, 1).wait_recv())
        pl.when(inner)(lambda: row_copy(stage, 3).start())
        row_copy(stage, 2).wait_recv()
        pl.when(outer)(lambda: row_copy(stage, 3).wait_recv())

    def row_drain(stage):
        pl.when(has_right)(lambda: row_copy(stage, 0).wait_send())
        pl.when(has_left)(lambda: row_copy(stage, 1).wait_send())
        row_copy(stage, 2).wait_send()
        pl.when(inner)(lambda: row_copy(stage, 3).wait_send())

    top, low = pl.ds(0, half), pl.ds(half, half)

    def col_copy(stage, i):
        t, m, y, g = term.at[stage], mid.at[stage], relayed.at[stage], got.at[stage]
        src, dst, device = (
            (t.at[2, top], m.at[0], col_right), (t.at[2, low], m.at[1], col_left),
            (t.at[1, low], g.at[0, low], col_right), (t.at[3, top], g.at[1, top], col_left),
            (y.at[0], g.at[0, top], col_right), (y.at[1], g.at[1, low], col_left))[i]
        return remote(src, dst, col_send.at[stage, i], col_recv.at[stage, i], device)

    row_start(0)
    for copy in loads[1:5]:
        copy.wait()
    me = r * blocks - 2 * blocks
    local = [jnp.clip(cols_s[s] - me, 0, 5 * blocks - 1) for s in range(slots)]
    for s in range(slots):
        live = s < count_s[0]
        for b in range(blocks):
            here = jnp.logical_and(live, rows_s[s] == b)
            keep = jnp.where(here, 1.0, 0.0).astype(BF16)
            placed[pl.ds(b * BS, BS), pl.ds(s * BS, BS)] = adj_v[s] * keep
    degree = jnp.dot(placed[...], jnp.ones((slots * BS, 2 * BS), BF16),
                     preferred_element_type=F32)
    scale[...] = lax.rsqrt(degree)

    def aggregate(stage):
        tiles = jnp.concatenate([ext[stage][i] for i in local], axis=0)
        summed = jnp.dot(placed[...], tiles, preferred_element_type=F32)
        return (summed * scale[...]).astype(BF16)

    def quarter(k):
        return pl.ds(pl.multiple_of(lax.rem(c + k, n_col) * node_rows, node_rows), node_rows)

    def self_project(stage, w_self):
        mine = jnp.concatenate([ext[stage][2 * blocks + b] for b in range(blocks)], axis=0)
        for k in range(n_col):
            self_term[stage, k] = jnp.dot(mine, w_self[:, quarter(k)],
                                          preferred_element_type=F32)

    def spread(stage, w_neigh):
        agg = aggregate(stage)
        for k, sent in ((2, (0, 1)), (1, (2,)), (3, (3,)), (0, ())):
            total = self_term[stage, k] + jnp.dot(
                agg, w_neigh[:, quarter(k)], preferred_element_type=F32)
            term[stage, k] = total.astype(BF16)
            for i in sent:
                col_copy(stage, i).start()

    def relay(stage):
        for i, mine in ((0, term[stage, 1, top]), (1, term[stage, 3, low])):
            col_copy(stage, i).wait_recv()
            both = mine.astype(F32) + mid[stage, i].astype(F32)
            relayed[stage, i] = both.astype(BF16)
            col_copy(stage, 4 + i).start()

    def gathered(stage):
        for i in range(2, 6):
            col_copy(stage, i).wait_recv()
        return (term[stage, 0].astype(F32) + got[stage, 0].astype(F32)
                + got[stage, 1].astype(F32))

    loads[5].wait()
    self_project(0, ws1)
    for copy in loads[6:]:
        copy.wait()
    row_wait(0)
    spread(0, wn1)
    for copy in mask_loads:
        copy.wait()
    relay(0)
    hidden = jnp.maximum(gathered(0), 0.0).astype(BF16)
    doubled = (hidden + hidden).astype(F32)
    for p in range(passes):
        dropped = (doubled * mask_v[p].astype(F32)).astype(BF16)
        for b in range(blocks):
            ext[1 + p][2 * blocks + b] = dropped[b * BS:(b + 1) * BS]
        row_start(1 + p)
    for p in range(passes):
        self_project(1 + p, ws2)
    for p in range(passes):
        row_wait(1 + p)
        spread(1 + p, wn2)
        if p:
            relay(p)
    for p in range(passes):
        if p == passes - 2:
            relay(passes)
        out[p] = gathered(1 + p).astype(BF16)
    for stage in range(1 + passes):
        row_drain(stage)
        for i in range(6):
            col_copy(stage, i).wait_send()


def interleave(stacked, out):
    passes, rows, _ = stacked.shape
    step = 32
    for low in range(0, rows, step):
        part = stacked[:, low:low + step, :].astype(F32)
        out[low:low + step] = jnp.swapaxes(part, 0, 1).astype(BF16)


def solution(mesh):
    n_row, n_col = mesh.shape["row"], mesh.shape["col"]

    def on_device(features, masks, adj, adj_rows, adj_cols, adj_count, *weights):
        node_rows, width = features.shape
        blocks, slots, passes = node_rows // BS, adj_rows.shape[0], masks.shape[1]
        hidden = weights[0].shape[1]
        dma = pltpu.SemaphoreType.DMA
        tile, halved = (node_rows, width), (node_rows // 2, width)
        ext = pltpu.VMEM((5 * blocks, BS, width), BF16)
        any_spec = pl.BlockSpec(memory_space=pl.ANY)
        vmem_spec = pl.BlockSpec(memory_space=pltpu.VMEM)
        stacked = pl.pallas_call(
            functools.partial(fused, n_row, n_col, passes, blocks, slots),
            out_shape=pltpu.VMEM((passes,) + tile, BF16),
            in_specs=[any_spec] * 10,
            out_specs=vmem_spec,
            scratch_shapes=[
                pltpu.SMEM((slots,), jnp.int32), pltpu.SMEM((slots,), jnp.int32),
                pltpu.SMEM((1,), jnp.int32),
                pltpu.VMEM(adj.shape, BF16), pltpu.VMEM((node_rows, slots * BS), BF16),
                pltpu.VMEM(tile, F32),
            ] + [pltpu.VMEM((width, hidden), BF16)] * 4 + [
                pltpu.VMEM((passes,) + tile, jnp.int32),
                pltpu.VMEM((1 + passes, n_col) + tile, F32),
                pltpu.VMEM((1 + passes, n_col) + tile, BF16),
                pltpu.VMEM((1 + passes, 2) + halved, BF16),
                pltpu.VMEM((1 + passes, 2) + halved, BF16),
                pltpu.VMEM((1 + passes, 2) + tile, BF16),
            ] + [ext] * (1 + passes) + [
                dma((9,)), dma((passes,)), dma((1 + passes, 4)), dma((1 + passes, 4)),
                dma((1 + passes, 6)), dma((1 + passes, 6)),
            ],
            compiler_params=pltpu.CompilerParams(
                collective_id=0, has_side_effects=True, vmem_limit_bytes=48 * 2**20),
        )(*[pltpu.with_memory_space_constraint(x, pltpu.HBM) if x.size > 1 else x for x in (
            features.reshape(blocks, BS, width), masks, adj, adj_rows, adj_cols, adj_count, *weights)])
        return pl.pallas_call(
            interleave,
            out_shape=jax.ShapeDtypeStruct((node_rows, passes, width), BF16),
            in_specs=[vmem_spec],
            out_specs=vmem_spec,
            compiler_params=pltpu.CompilerParams(vmem_limit_bytes=16 * 2**20),
        )(stacked)

    in_specs = (
        P("row", "col"), P("row", None, "col"), P("row", None, None), P("row"), P("row"),
        P("row"), P("col", None), P("col", None), P("col", None), P("col", None),
    )
    return jax.shard_map(on_device, mesh=mesh, in_specs=in_specs,
                         out_specs=P("row", None, "col"), check_vma=False)
```

time: 58.8 us -> 50.4 us (0.86)
  the two profiles are of different devices: /device:TPU:8 before, /device:TPU:103 now
where the time goes in v3:
time: 50.4 us; the launch traced here: 50.3 us
  Pallas kernels  49.7 us (99%)
  between operations  0.66 us (1%)
    pallas_call x1, Pallas kernels, on_device(): pl.pallas_call(functools.partial(fused, n_row, n_col, passes, blocks, slo...  48.6 us
    pallas_call x1, Pallas kernels, on_device(): pl.pallas_call(interleave, out_shape=jax.ShapeDtypeStruct((node_rows, pas...  1.07 us

profile of v3, /device:TPU:103, one launch (start us, length us, event | category | flops | bytes accessed | tf_op | source)
XLA Modules:
  0.0 50.3 jit_solution(6747700940121826657)
XLA Ops:
  0.7 48.6 %shard_map.100.stacked = bf16[4,256,256]{2,1,0:T(8,128)(2,1)S(1)} custom-call(bf16[2,128,256]{2,1,0:T(8,128)(2,1)} %bitcast.1, s32[256,4,256]{2,1,0:T(4,128)} %refs_1_.1, bf16[8,128,128]{2,1,0:T(8,128)(2,1)} %refs_2_.1, s32[8]{0:T(128)} %refs_3_.1, s32[8]{0:T(128)} %refs_4_.1, s32[1]{0:T(128)S(6)} %copy.11.refs_5_, bf16[256,1024]{1,0:T(8,128)(2,1)} %refs_6_.1, ...), custom_call_target="tpu_custom_call" | custom-call | tf_op jit(solution)/shard_map/pallas_call | solution.py:206
  49.3 1.1 %shard_map.101 = bf16[256,4,256]{2,1,0:T(4,128)(2,1)} custom-call(bf16[4,256,256]{2,1,0:T(8,128)(2,1)S(1)} %shard_map.100.stacked), custom_call_target="tpu_custom_call" | custom-call | tf_op jit(solution)/shard_map/pallas_call | solution.py:231

commit v4 on v3

--- a/solution.py
+++ b/solution.py
@@ -29,6 +29,7 @@
     sibling = (r + 1 - 2 * odd, c)
     far_right, far_left = (lax.rem(r + 2, n_row), c), (lax.rem(r + n_row - 2, n_row), c)
     col_right, col_left = (r, lax.rem(c + 1, n_col)), (r, lax.rem(c + n_col - 1, n_col))
+    neigh_stage, self_stage = passes, passes + 1
     node_rows = blocks * BS
     half = node_rows // 2
 
@@ -117,25 +118,32 @@
     def aggregate(stage):
         tiles = jnp.concatenate([ext[stage][i] for i in local], axis=0)
         summed = jnp.dot(placed[...], tiles, preferred_element_type=F32)
-        return (summed * scale[...]).astype(BF16)
+        return summed * scale[...]
 
     def quarter(k):
         return pl.ds(pl.multiple_of(lax.rem(c + k, n_col) * node_rows, node_rows), node_rows)
 
+    def own_rows(stage):
+        return jnp.concatenate([ext[stage][2 * blocks + b] for b in range(blocks)], axis=0)
+
+    def product(left, weight, k):
+        return jnp.dot(left, weight[:, quarter(k)], preferred_element_type=F32)
+
     def self_project(stage, w_self):
-        mine = jnp.concatenate([ext[stage][2 * blocks + b] for b in range(blocks)], axis=0)
+        mine = own_rows(stage)
         for k in range(n_col):
-            self_term[stage, k] = jnp.dot(mine, w_self[:, quarter(k)],
-                                          preferred_element_type=F32)
-
-    def spread(stage, w_neigh):
-        agg = aggregate(stage)
+            self_term[stage, k] = product(mine, w_self, k)
+
+    def spread(stage, share):
         for k, sent in ((2, (0, 1)), (1, (2,)), (3, (3,)), (0, ())):
-            total = self_term[stage, k] + jnp.dot(
-                agg, w_neigh[:, quarter(k)], preferred_element_type=F32)
-            term[stage, k] = total.astype(BF16)
+            term[stage, k] = share(k).astype(BF16)
             for i in sent:
                 col_copy(stage, i).start()
+
+    def spread_terms(row_stage, col_stage, w_neigh):
+        row_wait(row_stage)
+        agg = aggregate(row_stage).astype(BF16)
+        spread(col_stage, lambda k: self_term[row_stage, k] + product(agg, w_neigh, k))
 
     def relay(stage):
         for i, mine in ((0, term[stage, 1, top]), (1, term[stage, 3, low])):
@@ -154,31 +162,46 @@
     self_project(0, ws1)
     for copy in loads[6:]:
         copy.wait()
-    row_wait(0)
-    spread(0, wn1)
+    spread_terms(0, 0, wn1)
     for copy in mask_loads:
         copy.wait()
     relay(0)
     hidden = jnp.maximum(gathered(0), 0.0).astype(BF16)
     doubled = (hidden + hidden).astype(F32)
-    for p in range(passes):
-        dropped = (doubled * mask_v[p].astype(F32)).astype(BF16)
+
+    def dropped(p):
+        return (doubled * mask_v[p].astype(F32)).astype(BF16)
+
+    def send_rows(stage, value):
         for b in range(blocks):
-            ext[1 + p][2 * blocks + b] = dropped[b * BS:(b + 1) * BS]
-        row_start(1 + p)
-    for p in range(passes):
-        self_project(1 + p, ws2)
-    for p in range(passes):
-        row_wait(1 + p)
-        spread(1 + p, wn2)
-        if p:
-            relay(p)
-    for p in range(passes):
+            ext[stage][2 * blocks + b] = value[b * BS:(b + 1) * BS]
+        row_start(stage)
+
+    send_rows(1, dropped(1))
+    first = dropped(0)
+    spread(neigh_stage, lambda k: product(first, wn2, k))
+    spread(self_stage, lambda k: product(first, ws2, k))
+    for p in range(2, passes):
+        send_rows(p, dropped(p))
+    for p in range(1, passes):
+        self_project(p, ws2)
+    relay(neigh_stage)
+    relay(self_stage)
+    for p in range(1, passes):
+        spread_terms(p, p, wn2)
+        if p == 1:
+            send_rows(passes, gathered(neigh_stage).astype(BF16))
+        else:
+            relay(p - 1)
+    row_wait(passes)
+    out[0] = (gathered(self_stage) + aggregate(passes)).astype(BF16)
+    for p in range(1, passes):
         if p == passes - 2:
-            relay(passes)
-        out[p] = gathered(1 + p).astype(BF16)
+            relay(passes - 1)
+        out[p] = gathered(p).astype(BF16)
     for stage in range(1 + passes):
         row_drain(stage)
+    for stage in range(2 + passes):
         for i in range(6):
             col_copy(stage, i).wait_send()
 
@@ -215,14 +238,14 @@
                 pltpu.VMEM(tile, F32),
             ] + [pltpu.VMEM((width, hidden), BF16)] * 4 + [
                 pltpu.VMEM((passes,) + tile, jnp.int32),
-                pltpu.VMEM((1 + passes, n_col) + tile, F32),
-                pltpu.VMEM((1 + passes, n_col) + tile, BF16),
-                pltpu.VMEM((1 + passes, 2) + halved, BF16),
-                pltpu.VMEM((1 + passes, 2) + halved, BF16),
-                pltpu.VMEM((1 + passes, 2) + tile, BF16),
+                pltpu.VMEM((passes, n_col) + tile, F32),
+                pltpu.VMEM((2 + passes, n_col) + tile, BF16),
+                pltpu.VMEM((2 + passes, 2) + halved, BF16),
+                pltpu.VMEM((2 + passes, 2) + halved, BF16),
+                pltpu.VMEM((2 + passes, 2) + tile, BF16),
             ] + [ext] * (1 + passes) + [
                 dma((9,)), dma((passes,)), dma((1 + passes, 4)), dma((1 + passes, 4)),
-                dma((1 + passes, 6)), dma((1 + passes, 6)),
+                dma((2 + passes, 6)), dma((2 + passes, 6)),
             ],
             compiler_params=pltpu.CompilerParams(
                 collective_id=0, has_side_effects=True, vmem_limit_bytes=48 * 2**20),

time: 50.4 us -> 46.3 us (0.919)
  Pallas kernels: 49.7 us -> 45.6 us
    pallas_call x1, Pallas kernels: 48.6 us -> 44.5 us  [on_device(): pl.pallas_call(functools.partial(fused, n_row, n_col, passes, blocks, slo...]
where the time goes in v4:
time: 46.3 us; the launch traced here: 46.2 us
  Pallas kernels  45.6 us (98%)
  between operations  0.66 us (1%)
    pallas_call x1, Pallas kernels, on_device(): pl.pallas_call(functools.partial(fused, n_row, n_col, passes, blocks, slo...  44.5 us
    pallas_call x1, Pallas kernels, on_device(): pl.pallas_call(interleave, out_shape=jax.ShapeDtypeStruct((node_rows, pas...  1.07 us

profile of v4, /device:TPU:103, one launch (start us, length us, event | category | flops | bytes accessed | tf_op | source)
XLA Modules:
  0.0 46.2 jit_solution(15746372224904592155)
XLA Ops:
  0.7 44.5 %shard_map.100.stacked = bf16[4,256,256]{2,1,0:T(8,128)(2,1)S(1)} custom-call(bf16[2,128,256]{2,1,0:T(8,128)(2,1)} %bitcast.1, s32[256,4,256]{2,1,0:T(4,128)} %refs_1_.1, bf16[8,128,128]{2,1,0:T(8,128)(2,1)} %refs_2_.1, s32[8]{0:T(128)} %refs_3_.1, s32[8]{0:T(128)} %refs_4_.1, s32[1]{0:T(128)S(6)} %copy.11.refs_5_, bf16[256,1024]{1,0:T(8,128)(2,1)} %refs_6_.1, ...), custom_call_target="tpu_custom_call" | custom-call | tf_op jit(solution)/shard_map/pallas_call | solution.py:229
  45.2 1.1 %shard_map.101 = bf16[256,4,256]{2,1,0:T(4,128)(2,1)} custom-call(bf16[4,256,256]{2,1,0:T(8,128)(2,1)S(1)} %shard_map.100.stacked), custom_call_target="tpu_custom_call" | custom-call | tf_op jit(solution)/shard_map/pallas_call | solution.py:254

commit v5 on v4

--- a/solution.py
+++ b/solution.py
@@ -12,14 +12,15 @@
 BF16, F32 = jnp.bfloat16, jnp.float32
 
 
-def fused(n_row, n_col, passes, blocks, slots, *refs):
+def fused(n_row, n_col, passes, wide, blocks, slots, *refs):
     (features, masks, adj, adj_rows, adj_cols, adj_count, w_self_one, w_neigh_one,
      w_self_two, w_neigh_two, out) = refs[:11]
     rest = list(refs[11:])
-    rows_s, cols_s, count_s, adj_v, placed, scale, ws1, wn1, ws2, wn2, mask_v = rest[:11]
-    self_term, term, mid, relayed, got = rest[11:16]
-    ext = rest[16:17 + passes]
-    load_sem, mask_sem, row_send, row_recv, col_send, col_recv = rest[17 + passes:]
+    rows_s, cols_s, count_s, adj_v, placed, scale, ws1, wn1, w2, mask_v = rest[:10]
+    self_term, term, mid, relayed, got, spread_w, shared, self_wide = rest[10:18]
+    ext = rest[18:19 + passes]
+    (load_sem, mask_sem, row_send, row_recv, col_send, col_recv, share_send, share_recv,
+     w_send, w_recv) = rest[19 + passes:]
 
     r, c = lax.axis_index("row"), lax.axis_index("col")
     odd = lax.rem(r, 2)
@@ -29,7 +30,8 @@
     sibling = (r + 1 - 2 * odd, c)
     far_right, far_left = (lax.rem(r + 2, n_row), c), (lax.rem(r + n_row - 2, n_row), c)
     col_right, col_left = (r, lax.rem(c + 1, n_col)), (r, lax.rem(c + n_col - 1, n_col))
-    neigh_stage, self_stage = passes, passes + 1
+    narrow = range(wide, passes)
+    col_across = (r, lax.rem(c + 2, n_col))
     node_rows = blocks * BS
     half = node_rows // 2
 
@@ -40,15 +42,15 @@
 
     pl.when(has_right)(lambda: greet(far_right))
     pl.when(has_left)(lambda: greet(far_left))
-    for device in (sibling, col_right, col_left):
+    for device in (sibling, col_right, col_left, col_across):
         greet(device)
 
     loads = []
     own = ext[0].at[pl.ds(2 * blocks, blocks)]
     for i, (src, dst) in enumerate(
         ((features, own), (adj, adj_v), (adj_rows, rows_s), (adj_cols, cols_s),
-         (adj_count, count_s), (w_self_one, ws1), (w_neigh_one, wn1), (w_self_two, ws2),
-         (w_neigh_two, wn2))
+         (adj_count, count_s), (w_self_one, ws1), (w_neigh_one, wn1), (w_self_two, w2.at[0]),
+         (w_neigh_two, w2.at[1]))
     ):
         loads.append(pltpu.make_async_copy(src, dst, load_sem.at[i]))
     mask_loads = [
@@ -58,7 +60,7 @@
     for copy in loads + mask_loads:
         copy.start()
     loads[0].wait()
-    pl.semaphore_wait(barrier, 3 + has_left.astype(jnp.int32) + has_right.astype(jnp.int32))
+    pl.semaphore_wait(barrier, 4 + has_left.astype(jnp.int32) + has_right.astype(jnp.int32))
 
     def remote(src, dst, send, recv, device):
         return pltpu.make_async_remote_copy(
@@ -100,7 +102,52 @@
             (y.at[0], g.at[0, top], col_right), (y.at[1], g.at[1, low], col_left))[i]
         return remote(src, dst, col_send.at[stage, i], col_recv.at[stage, i], device)
 
+    def share_copy(stage, i):
+        held = shared.at[stage]
+        src, dst, device = (
+            (held.at[0, top], held.at[1, top], col_right),
+            (held.at[0, low], held.at[3, low], col_left),
+            (held.at[0, low], held.at[1, low], col_right),
+            (held.at[0, top], held.at[3, top], col_left),
+            (held.at[1, top], held.at[2, top], col_right),
+            (held.at[3, low], held.at[2, low], col_left))[i]
+        return remote(src, dst, share_send.at[stage, i], share_recv.at[stage, i], device)
+
+    def share_start(stage, *which):
+        for i in which:
+            share_copy(stage, i).start()
+
+    def share_forward(stage):
+        for i in (0, 1):
+            share_copy(stage, i).wait_recv()
+            share_copy(stage, 4 + i).start()
+
+    def share_wait(stage):
+        for i in range(2, 6):
+            share_copy(stage, i).wait_recv()
+
+    def quarter(k):
+        return pl.ds(pl.multiple_of(lax.rem(c + k, n_col) * node_rows, node_rows), node_rows)
+
+    def weight_copy(k):
+        device = {1: col_right, 2: col_across, 3: col_left}[k]
+        return remote(w2.at[odd, :, quarter(k)], spread_w.at[odd, k - 1],
+                      w_send.at[0, k - 1], w_recv.at[0, k - 1], device)
+
+    def weight_forward(k):
+        block = spread_w.at[odd, k - 1]
+        return remote(block, block, w_send.at[1, k - 1], w_recv.at[1, k - 1], sibling)
+
     row_start(0)
+    for copy in loads[7:]:
+        copy.wait()
+    for k in (2, 1, 3):
+        weight_copy(k).start()
+    for copy in mask_loads[:wide]:
+        copy.wait()
+    for p in range(wide):
+        shared[p, 0] = (2 * mask_v[p]).astype(BF16)
+    share_start(0, 0, 1)
     for copy in loads[1:5]:
         copy.wait()
     me = r * blocks - 2 * blocks
@@ -120,14 +167,14 @@
         summed = jnp.dot(placed[...], tiles, preferred_element_type=F32)
         return summed * scale[...]
 
-    def quarter(k):
-        return pl.ds(pl.multiple_of(lax.rem(c + k, n_col) * node_rows, node_rows), node_rows)
-
     def own_rows(stage):
         return jnp.concatenate([ext[stage][2 * blocks + b] for b in range(blocks)], axis=0)
 
     def product(left, weight, k):
         return jnp.dot(left, weight[:, quarter(k)], preferred_element_type=F32)
+
+    def matmul(left, right):
+        return jnp.dot(left, right, preferred_element_type=F32)
 
     def self_project(stage, w_self):
         mine = own_rows(stage)
@@ -160,50 +207,75 @@
 
     loads[5].wait()
     self_project(0, ws1)
-    for copy in loads[6:]:
-        copy.wait()
+    loads[6].wait()
     spread_terms(0, 0, wn1)
-    for copy in mask_loads:
+    share_start(1, 0, 1)
+    for copy in mask_loads[wide:]:
         copy.wait()
     relay(0)
+    share_start(0, 2, 3)
+    for k in (1, 3, 2):
+        weight_copy(k).wait_recv()
+        weight_forward(k).start()
+    share_forward(0)
     hidden = jnp.maximum(gathered(0), 0.0).astype(BF16)
     doubled = (hidden + hidden).astype(F32)
-
-    def dropped(p):
-        return (doubled * mask_v[p].astype(F32)).astype(BF16)
 
     def send_rows(stage, value):
         for b in range(blocks):
             ext[stage][2 * blocks + b] = value[b * BS:(b + 1) * BS]
         row_start(stage)
 
-    send_rows(1, dropped(1))
-    first = dropped(0)
-    spread(neigh_stage, lambda k: product(first, wn2, k))
-    spread(self_stage, lambda k: product(first, ws2, k))
-    for p in range(2, passes):
-        send_rows(p, dropped(p))
-    for p in range(1, passes):
-        self_project(p, ws2)
-    relay(neigh_stage)
-    relay(self_stage)
-    for p in range(1, passes):
-        spread_terms(p, p, wn2)
-        if p == 1:
-            send_rows(passes, gathered(neigh_stage).astype(BF16))
-        else:
-            relay(p - 1)
-    row_wait(passes)
-    out[0] = (gathered(self_stage) + aggregate(passes)).astype(BF16)
-    for p in range(1, passes):
-        if p == passes - 2:
-            relay(passes - 1)
-        out[p] = gathered(p).astype(BF16)
+    def send_dropped(p):
+        send_rows(1 + p, (doubled * mask_v[p].astype(F32)).astype(BF16))
+
+    send_dropped(wide)
+    shared[wide, 0] = hidden
+    share_start(wide, 0, 1, 2, 3)
+    for p in narrow[1:]:
+        send_dropped(p)
+    for p in range(1, wide):
+        share_start(p, 2, 3)
+    for p in narrow:
+        self_project(1 + p, w2.at[0])
+    for stage in range(wide, 0, -1):
+        share_forward(stage)
+    for k in (1, 3, 2):
+        weight_forward(k).wait_recv()
+
+    def project_wide(p):
+        share_wait(p)
+        totals = [jnp.zeros((node_rows, node_rows), F32)] * 2
+        for k in range(n_col):
+            kept = (shared[wide, k].astype(F32) * shared[p, k].astype(F32)).astype(BF16)
+            for m in range(2):
+                block = spread_w[m, k - 1] if k else w2[m, :, quarter(0)]
+                totals[m] = totals[m] + matmul(kept, block)
+        self_wide[p] = totals[0]
+        send_rows(1 + p, totals[1].astype(BF16))
+
+    for i, p in enumerate(narrow):
+        spread_terms(1 + p, 1 + i, w2.at[1])
+        if i == 0:
+            share_wait(wide)
+        project_wide(i)
+    for i, p in enumerate(narrow):
+        relay(1 + i)
+    for p in range(wide):
+        row_wait(1 + p)
+        out[p] = (self_wide[p] + aggregate(1 + p)).astype(BF16)
+    for i, p in enumerate(narrow):
+        out[p] = gathered(1 + i).astype(BF16)
     for stage in range(1 + passes):
         row_drain(stage)
-    for stage in range(2 + passes):
-        for i in range(6):
+    for i in range(6):
+        for stage in range(1 + len(narrow)):
             col_copy(stage, i).wait_send()
+        for stage in range(1 + wide):
+            share_copy(stage, i).wait_send()
+    for k in range(1, n_col):
+        weight_copy(k).wait_send()
+        weight_forward(k).wait_send()
 
 
 def interleave(stacked, out):
@@ -221,13 +293,15 @@
         node_rows, width = features.shape
         blocks, slots, passes = node_rows // BS, adj_rows.shape[0], masks.shape[1]
         hidden = weights[0].shape[1]
+        wide = passes // 2
+        scatters = 1 + passes - wide
         dma = pltpu.SemaphoreType.DMA
         tile, halved = (node_rows, width), (node_rows // 2, width)
         ext = pltpu.VMEM((5 * blocks, BS, width), BF16)
         any_spec = pl.BlockSpec(memory_space=pl.ANY)
         vmem_spec = pl.BlockSpec(memory_space=pltpu.VMEM)
         stacked = pl.pallas_call(
-            functools.partial(fused, n_row, n_col, passes, blocks, slots),
+            functools.partial(fused, n_row, n_col, passes, wide, blocks, slots),
             out_shape=pltpu.VMEM((passes,) + tile, BF16),
             in_specs=[any_spec] * 10,
             out_specs=vmem_spec,
@@ -236,16 +310,21 @@
                 pltpu.SMEM((1,), jnp.int32),
                 pltpu.VMEM(adj.shape, BF16), pltpu.VMEM((node_rows, slots * BS), BF16),
                 pltpu.VMEM(tile, F32),
-            ] + [pltpu.VMEM((width, hidden), BF16)] * 4 + [
+                pltpu.VMEM((width, hidden), BF16), pltpu.VMEM((width, hidden), BF16),
+                pltpu.VMEM((2, width, hidden), BF16),
                 pltpu.VMEM((passes,) + tile, jnp.int32),
-                pltpu.VMEM((passes, n_col) + tile, F32),
-                pltpu.VMEM((2 + passes, n_col) + tile, BF16),
-                pltpu.VMEM((2 + passes, 2) + halved, BF16),
-                pltpu.VMEM((2 + passes, 2) + halved, BF16),
-                pltpu.VMEM((2 + passes, 2) + tile, BF16),
+                pltpu.VMEM((1 + passes, n_col) + tile, F32),
+                pltpu.VMEM((scatters, n_col) + tile, BF16),
+                pltpu.VMEM((scatters, 2) + halved, BF16),
+                pltpu.VMEM((scatters, 2) + halved, BF16),
+                pltpu.VMEM((scatters, 2) + tile, BF16),
+                pltpu.VMEM((2, n_col - 1) + tile, BF16),
+                pltpu.VMEM((1 + wide, n_col) + tile, BF16),
+                pltpu.VMEM((wide,) + tile, F32),
             ] + [ext] * (1 + passes) + [
                 dma((9,)), dma((passes,)), dma((1 + passes, 4)), dma((1 + passes, 4)),
-                dma((2 + passes, 6)), dma((2 + passes, 6)),
+                dma((scatters, 6)), dma((scatters, 6)), dma((1 + wide, 6)),
+                dma((1 + wide, 6)), dma((2, n_col - 1)), dma((2, n_col - 1)),
             ],
             compiler_params=pltpu.CompilerParams(
                 collective_id=0, has_side_effects=True, vmem_limit_bytes=48 * 2**20),

time: 46.3 us -> 44.1 us (0.952)
  Pallas kernels: 45.6 us -> 43.4 us
    pallas_call x1, Pallas kernels: 44.5 us -> 42.3 us  [on_device(): pl.pallas_call(functools.partial(fused, n_row, n_col, passes, wide, block...]
where the time goes in v5:
time: 44.1 us; the launch traced here: 44 us
  Pallas kernels  43.4 us (98%)
  between operations  0.66 us (1%)
    pallas_call x1, Pallas kernels, on_device(): pl.pallas_call(functools.partial(fused, n_row, n_col, passes, wide, block...  42.3 us
    pallas_call x1, Pallas kernels, on_device(): pl.pallas_call(interleave, out_shape=jax.ShapeDtypeStruct((node_rows, pas...  1.07 us

profile of v5, /device:TPU:103, one launch (start us, length us, event | category | flops | bytes accessed | tf_op | source)
XLA Modules:
  0.0 44.0 jit_solution(12230276531650812746)
XLA Ops:
  0.7 42.3 %shard_map.100.stacked = bf16[4,256,256]{2,1,0:T(8,128)(2,1)S(1)} custom-call(bf16[2,128,256]{2,1,0:T(8,128)(2,1)} %bitcast.1, s32[256,4,256]{2,1,0:T(4,128)} %refs_1_.1, bf16[8,128,128]{2,1,0:T(8,128)(2,1)} %refs_2_.1, s32[8]{0:T(128)} %refs_3_.1, s32[8]{0:T(128)} %refs_4_.1, s32[1]{0:T(128)S(6)} %copy.11.refs_5_, bf16[256,1024]{1,0:T(8,128)(2,1)} %refs_6_.1, ...), custom_call_target="tpu_custom_call" | custom-call | tf_op jit(solution)/shard_map/pallas_call | solution.py:303
  43.0 1.1 %shard_map.101 = bf16[256,4,256]{2,1,0:T(4,128)(2,1)} custom-call(bf16[4,256,256]{2,1,0:T(8,128)(2,1)S(1)} %shard_map.100.stacked), custom_call_target="tpu_custom_call" | custom-call | tf_op jit(solution)/shard_map/pallas_call | solution.py:333

commit v6 on v5

v6 whole, which is shorter than its diff:
```python
import functools

import jax
import jax.numpy as jnp
from jax import lax
from jax.experimental import pallas as pl
from jax.experimental.pallas import tpu as pltpu
from jax.sharding import PartitionSpec as P

BS = 128
LINE = 4
MESH = pl.DeviceIdType.MESH
BF16, F32 = jnp.bfloat16, jnp.float32


def fused(n_row, n_col, passes, wide, blocks, slots, *refs):
    (features, masks, adj, adj_rows, adj_cols, adj_count, w_self_one, w_neigh_one,
     w_self_two, w_neigh_two, out) = refs[:11]
    rest = list(refs[11:])
    rows_s, cols_s, count_s, adj_v, placed, scale, ws1, wn1, w2, mask_v = rest[:10]
    self_term, term, mid, relayed, got, spread_w, shared, self_wide = rest[10:18]
    ext = rest[18:19 + passes]
    (load_sem, row_send, far_recv, near_recv, col_send, col_recv, share_send, share_recv,
     w_send, w_recv) = rest[19 + passes:]

    r, c = lax.axis_index("row"), lax.axis_index("col")
    odd = lax.rem(r, 2)
    has_left, has_right = r >= 2, r < n_row - 2
    inner = jnp.where(odd == 0, has_right, has_left)
    outer = jnp.where(odd == 0, has_left, has_right)
    sibling = (r + 1 - 2 * odd, c)
    far_right, far_left = (lax.rem(r + 2, n_row), c), (lax.rem(r + n_row - 2, n_row), c)
    col_right, col_left = (r, lax.rem(c + 1, n_col)), (r, lax.rem(c + n_col - 1, n_col))
    narrow = range(wide, passes)
    row_parts = [2 if stage == 1 + wide else 1 for stage in range(1 + passes)]
    col_across = (r, lax.rem(c + 2, n_col))
    node_rows = blocks * BS
    piece, tall = node_rows // 4, node_rows // 2
    line = 2 * LINE
    spot = lax.rem(r // 2, LINE)

    barrier = pltpu.get_barrier_semaphore()

    def greet(device):
        pl.semaphore_signal(barrier, 1, device_id=device, device_id_type=MESH)

    pl.when(has_right)(lambda: greet(far_right))
    pl.when(has_left)(lambda: greet(far_left))
    def along_line(by):
        return (r - lax.rem(r, line) + lax.rem(r + 2 * by, line), c)

    for device in (sibling, col_right, col_left, col_across) + tuple(
            along_line(by) for by in range(1, LINE)):
        greet(device)

    loads = []
    own = ext[0].at[pl.ds(2 * blocks, blocks)]
    for i, src, dst in (
        (0, features, own), (1, adj, adj_v), (2, adj_rows, rows_s), (3, adj_cols, cols_s),
        (4, adj_count, count_s), (5, w_self_one, ws1), (6, w_neigh_one, wn1),
        (7, w_self_two, w2.at[0]), (7, w_neigh_two, w2.at[1]),
    ):
        loads.append(pltpu.make_async_copy(src, dst, load_sem.at[i]))
    mask_loads = [
        pltpu.make_async_copy(masks.at[:, p, :], mask_v.at[p], load_sem.at[8])
        for p in range(passes)
    ]

    def wait_for(ref, sem):
        pltpu.make_async_copy(ref, ref, sem).wait()

    for copy in loads + mask_loads:
        copy.start()
    loads[0].wait()
    pl.semaphore_wait(
        barrier, 3 + LINE + has_left.astype(jnp.int32) + has_right.astype(jnp.int32))

    def remote(src, dst, send, recv, device):
        return pltpu.make_async_remote_copy(
            src_ref=src, dst_ref=dst, send_sem=send, recv_sem=recv, device_id=device,
            device_id_type=MESH)

    def row_copy(stage, i, part):
        src, dst, device = (
            (2, 0, far_right), (2, 4, far_left), (2, 1 + 2 * odd, sibling),
            (4 - 4 * odd, 3 - 2 * odd, sibling))[i]
        size = blocks // row_parts[stage]
        pairs = [ext[stage].at[pl.ds(n * blocks + part * size, size)] for n in (src, dst)]
        recv = far_recv.at[stage, part] if i < 2 else near_recv.at[stage]
        return remote(*pairs, row_send.at[stage], recv, device)

    def row_start(stage, part):
        pl.when(has_right)(lambda: row_copy(stage, 0, part).start())
        pl.when(has_left)(lambda: row_copy(stage, 1, part).start())
        row_copy(stage, 2, part).start()

    def one_of(flag, stage, many, few, sem):
        pl.when(flag)(lambda: wait_for(ext[stage].at[pl.ds(0, many)], sem))
        pl.when(jnp.logical_not(flag))(lambda: wait_for(ext[stage].at[pl.ds(0, few)], sem))

    both = jnp.logical_and(has_left, has_right)

    def row_wait(stage):
        size = blocks // row_parts[stage]
        for part in range(row_parts[stage]):
            one_of(both, stage, 2 * size, size, far_recv.at[stage, part])
            pl.when(inner)(lambda: row_copy(stage, 3, part).start())
        one_of(outer, stage, 2 * blocks, blocks, near_recv.at[stage])

    def row_drain(stage):
        sent = row_send.at[stage]
        pl.when(both)(lambda: wait_for(ext[stage].at[pl.ds(0, 4 * blocks)], sent))

        @pl.when(jnp.logical_not(both))
        def _():
            one_of(inner, stage, 3 * blocks, 2 * blocks, sent)

    def rows(j):
        return pl.ds(j * piece, piece)

    def toward(j):
        return (col_right, col_left)[j % 2]

    def onward(j):
        return (1, 3)[j % 2]

    def col_copy(stage, i):
        t, g = term.at[stage], got.at[stage]
        j = i % 4
        if i < 4:
            src, dst, device = t.at[2, rows(j)], mid.at[stage, rows(j)], toward(j)
        elif i < 8:
            src, dst, device = relayed.at[stage, rows(j)], g.at[j % 2, rows(j)], toward(j)
        else:
            k = 4 - onward(j)
            src, dst, device = t.at[k, rows(j)], g.at[1 - j % 2, rows(j)], toward(j + 1)
        recv = col_recv.at[stage, 0 if i < 4 else 1, j // 2]
        return remote(src, dst, col_send.at[stage], recv, device)

    def share_copy(stage, i):
        held = shared.at[stage]
        j = i % 4
        if i < 4:
            src, dst, device = 0, onward(j), toward(j)
        elif i < 8:
            src, dst, device = 0, 4 - onward(j), toward(j + 1)
        else:
            src, dst, device = onward(j), 2, toward(j)
        return remote(held.at[src, rows(j)], held.at[dst, rows(j)], share_send.at[stage],
                      share_recv.at[stage, j // 2 if i < 4 else 2], device)

    def share_start(stage, *which):
        for i in which:
            share_copy(stage, i).start()

    def tall_rows(part):
        return pl.ds(part * tall, tall)

    def share_forward(stage):
        for part in (0, 1):
            wait_for(shared.at[stage, 1, tall_rows(part)], share_recv.at[stage, part])
            share_start(stage, 8 + 2 * part, 9 + 2 * part)

    def share_wait(stage):
        wait_for(shared.at[stage, pl.ds(1, 2)], share_recv.at[stage, 2])

    def quarter(k):
        return pl.ds(pl.multiple_of(lax.rem(c + k, n_col) * node_rows, node_rows), node_rows)

    part_rows = pl.ds(pl.multiple_of(spot * piece, piece), piece)

    def weight_copy(k):
        device = {1: col_right, 2: col_across, 3: col_left}[k]
        return remote(w2.at[odd, part_rows, quarter(k)], spread_w.at[odd, k - 1, part_rows],
                      w_send.at[0], w_recv.at[0], device)

    def line_copy(by):
        part = spread_w.at[odd, :, part_rows]
        return remote(part, part, w_send.at[1], w_recv.at[1], along_line(by))

    def weight_forward():
        blocks_held = spread_w.at[odd]
        return remote(blocks_held, blocks_held, w_send.at[2], w_recv.at[2], sibling)

    row_start(0, 0)
    wait_for(w2, load_sem.at[7])
    for k in (2, 1, 3):
        weight_copy(k).start()
    wait_for(mask_v, load_sem.at[8])
    for p in range(wide):
        shared[p, 0] = (2 * mask_v[p]).astype(BF16)
    share_start(0, 0, 1, 2, 3, 4, 5, 6, 7)
    share_start(1, 0, 1, 2, 3)
    for copy in loads[1:5]:
        copy.wait()
    me = r * blocks - 2 * blocks
    local = [jnp.clip(cols_s[s] - me, 0, 5 * blocks - 1) for s in range(slots)]
    for s in range(slots):
        live = s < count_s[0]
        for b in range(blocks):
            here = jnp.logical_and(live, rows_s[s] == b)
            keep = jnp.where(here, 1.0, 0.0).astype(BF16)
            placed[pl.ds(b * BS, BS), pl.ds(s * BS, BS)] = adj_v[s] * keep
    degree = jnp.dot(placed[...], jnp.ones((slots * BS, 2 * BS), BF16),
                     preferred_element_type=F32)
    scale[...] = lax.rsqrt(degree)

    def aggregate(stage):
        tiles = jnp.concatenate([ext[stage][i] for i in local], axis=0)
        summed = jnp.dot(placed[...], tiles, preferred_element_type=F32)
        return summed * scale[...]

    def own_rows(stage):
        return jnp.concatenate([ext[stage][2 * blocks + b] for b in range(blocks)], axis=0)

    def product(left, weight, k):
        return jnp.dot(left, weight[:, quarter(k)], preferred_element_type=F32)

    def matmul(left, right):
        return jnp.dot(left, right, preferred_element_type=F32)

    def self_project(stage, w_self):
        mine = own_rows(stage)
        for k in range(n_col):
            self_term[stage, k] = product(mine, w_self, k)

    def spread(stage, share):
        for k, sent in ((2, (0, 1, 2, 3)), (1, (9, 11)), (3, (8, 10)), (0, ())):
            term[stage, k] = share(k).astype(BF16)
            for i in sent:
                col_copy(stage, i).start()

    def spread_terms(row_stage, col_stage, w_neigh):
        row_wait(row_stage)
        agg = aggregate(row_stage).astype(BF16)
        spread(col_stage, lambda k: self_term[row_stage, k] + product(agg, w_neigh, k))

    def relay(stage, part):
        wait_for(mid.at[stage, tall_rows(part)], col_recv.at[stage, 0, part])
        for j in (2 * part, 2 * part + 1):
            both_terms = (term[stage, onward(j), rows(j)].astype(F32)
                          + mid[stage, rows(j)].astype(F32))
            relayed[stage, rows(j)] = both_terms.astype(BF16)
            col_copy(stage, 4 + j).start()

    def gathered(stage, part):
        wait_for(got.at[stage, :, tall_rows(part)], col_recv.at[stage, 1, part])
        here = tall_rows(part)
        return (term[stage, 0, here].astype(F32) + got[stage, 0, here].astype(F32)
                + got[stage, 1, here].astype(F32))

    loads[5].wait()
    self_project(0, ws1)
    loads[6].wait()
    spread_terms(0, 0, wn1)
    wait_for(spread_w.at[odd, :, part_rows], w_recv.at[0])
    for by in (2, 1, 3):
        line_copy(by).start()
    for part in (0, 1):
        relay(0, part)
    share_start(1, 4, 5, 6, 7)
    share_forward(0)

    def send_dropped(p, part):
        kept = (shared[wide, 0, tall_rows(part)].astype(F32)
                * (2 * mask_v[p, tall_rows(part)]).astype(F32)).astype(BF16)
        for b in range(blocks // 2):
            ext[1 + p][2 * blocks + part * (blocks // 2) + b] = kept[b * BS:(b + 1) * BS]

    for part in (0, 1):
        shared[wide, 0, tall_rows(part)] = jnp.maximum(gathered(0, part), 0.0).astype(BF16)
        share_start(wide, 2 * part, 2 * part + 1)
        send_dropped(wide, part)
        row_start(1 + wide, part)
    share_start(wide, 4, 5, 6, 7)
    for p in narrow[1:]:
        for part in (0, 1):
            send_dropped(p, part)
        row_start(1 + p, 0)
    share_forward(wide)
    share_forward(1)
    wait_for(spread_w.at[odd, :, pl.ds(0, 3 * piece)], w_recv.at[1])
    weight_forward().start()
    for p in narrow:
        self_project(1 + p, w2.at[0])

    def project_wide(p):
        share_wait(p)
        kept = [(shared[wide, k].astype(F32) * shared[p, k].astype(F32)).astype(BF16)
                for k in range(n_col)]

        def project(m):
            total = product(kept[0], w2.at[m], 0)
            for k in range(1, n_col):
                total = total + matmul(kept[k], spread_w[m, k - 1])
            return total

        value = project(1).astype(BF16)
        for b in range(blocks):
            ext[1 + p][2 * blocks + b] = value[b * BS:(b + 1) * BS]
        row_start(1 + p, 0)
        self_wide[p] = project(0)

    for i, p in enumerate(narrow):
        spread_terms(1 + p, 1 + i, w2.at[1])
        if i == 0:
            share_wait(wide)
            weight_forward().wait_recv()
        project_wide(i)
    for i, p in enumerate(narrow):
        for part in (0, 1):
            relay(1 + i, part)
    for p in range(wide):
        row_wait(1 + p)
        out[p] = (self_wide[p] + aggregate(1 + p)).astype(BF16)
    for i, p in enumerate(narrow):
        for part in (0, 1):
            out[p, tall_rows(part)] = gathered(1 + i, part).astype(BF16)
    for stage in range(1 + passes):
        row_drain(stage)
    for stage in range(1 + len(narrow)):
        wait_for(term.at[stage, pl.ds(0, 3)], col_send.at[stage])
    for stage in range(1 + wide):
        wait_for(shared.at[stage, pl.ds(0, 3)], share_send.at[stage])
    wait_for(spread_w.at[odd, :, part_rows], w_send.at[0])
    wait_for(spread_w.at[odd, :, pl.ds(0, 3 * piece)], w_send.at[1])
    wait_for(spread_w.at[odd], w_send.at[2])


def interleave(stacked, out):
    passes, rows, _ = stacked.shape
    step = 32
    for low in range(0, rows, step):
        part = stacked[:, low:low + step, :].astype(F32)
        out[low:low + step] = jnp.swapaxes(part, 0, 1).astype(BF16)


def solution(mesh):
    n_row, n_col = mesh.shape["row"], mesh.shape["col"]

    def on_device(features, masks, adj, adj_rows, adj_cols, adj_count, *weights):
        node_rows, width = features.shape
        blocks, slots, passes = node_rows // BS, adj_rows.shape[0], masks.shape[1]
        hidden = weights[0].shape[1]
        wide = passes // 2
        scatters = 1 + passes - wide
        dma = pltpu.SemaphoreType.DMA
        tile = (node_rows, width)
        ext = pltpu.VMEM((5 * blocks, BS, width), BF16)
        any_spec = pl.BlockSpec(memory_space=pl.ANY)
        vmem_spec = pl.BlockSpec(memory_space=pltpu.VMEM)
        stacked = pl.pallas_call(
            functools.partial(fused, n_row, n_col, passes, wide, blocks, slots),
            out_shape=pltpu.VMEM((passes,) + tile, BF16),
            in_specs=[any_spec] * 10,
            out_specs=vmem_spec,
            scratch_shapes=[
                pltpu.SMEM((slots,), jnp.int32), pltpu.SMEM((slots,), jnp.int32),
                pltpu.SMEM((1,), jnp.int32),
                pltpu.VMEM(adj.shape, BF16), pltpu.VMEM((node_rows, slots * BS), BF16),
                pltpu.VMEM(tile, F32),
                pltpu.VMEM((width, hidden), BF16), pltpu.VMEM((width, hidden), BF16),
                pltpu.VMEM((2, width, hidden), BF16),
                pltpu.VMEM((passes,) + tile, jnp.int32),
                pltpu.VMEM((1 + passes, n_col) + tile, F32),
                pltpu.VMEM((scatters, n_col) + tile, BF16),
                pltpu.VMEM((scatters,) + tile, BF16),
                pltpu.VMEM((scatters,) + tile, BF16),
                pltpu.VMEM((scatters, 2) + tile, BF16),
                pltpu.VMEM((2, n_col - 1) + tile, BF16),
                pltpu.VMEM((1 + wide, n_col) + tile, BF16),
                pltpu.VMEM((wide,) + tile, F32),
            ] + [ext] * (1 + passes) + [
                dma((9,)), dma((1 + passes,)), dma((1 + passes, 2)), dma((1 + passes,)),
                dma((scatters,)), dma((scatters, 2, 2)), dma((1 + wide,)),
                dma((1 + wide, 3)), dma((3,)), dma((3,)),
            ],
            compiler_params=pltpu.CompilerParams(
                collective_id=0, has_side_effects=True, vmem_limit_bytes=48 * 2**20),
        )(*[pltpu.with_memory_space_constraint(x, pltpu.HBM) if x.size > 1 else x for x in (
            features.reshape(blocks, BS, width), masks, adj, adj_rows, adj_cols, adj_count, *weights)])
        return pl.pallas_call(
            interleave,
            out_shape=jax.ShapeDtypeStruct((node_rows, passes, width), BF16),
            in_specs=[vmem_spec],
            out_specs=vmem_spec,
            compiler_params=pltpu.CompilerParams(vmem_limit_bytes=16 * 2**20),
        )(stacked)

    in_specs = (
        P("row", "col"), P("row", None, "col"), P("row", None, None), P("row"), P("row"),
        P("row"), P("col", None), P("col", None), P("col", None), P("col", None),
    )
    return jax.shard_map(on_device, mesh=mesh, in_specs=in_specs,
                         out_specs=P("row", None, "col"), check_vma=False)
```

time: 44.1 us -> 41.6 us (0.943)
  Pallas kernels: 43.4 us -> 40.8 us
    pallas_call x1, Pallas kernels: 42.3 us -> 39.7 us  [on_device(): pl.pallas_call(functools.partial(fused, n_row, n_col, passes, wide, block...]
where the time goes in v6:
time: 41.6 us; the launch traced here: 41.4 us
  Pallas kernels  40.8 us (98%)
  between operations  0.66 us (2%)
    pallas_call x1, Pallas kernels, on_device(): pl.pallas_call(functools.partial(fused, n_row, n_col, passes, wide, block...  39.7 us
    pallas_call x1, Pallas kernels, on_device(): pl.pallas_call(interleave, out_shape=jax.ShapeDtypeStruct((node_rows, pas...  1.07 us

profile of v6, /device:TPU:103, one launch (start us, length us, event | category | flops | bytes accessed | tf_op | source)
XLA Modules:
  0.0 41.4 jit_solution(3457232471016473845)
XLA Ops:
  0.7 39.7 %shard_map.100.stacked = bf16[4,256,256]{2,1,0:T(8,128)(2,1)S(1)} custom-call(bf16[2,128,256]{2,1,0:T(8,128)(2,1)} %bitcast.1, s32[256,4,256]{2,1,0:T(4,128)} %refs_1_.1, bf16[8,128,128]{2,1,0:T(8,128)(2,1)} %refs_2_.1, s32[8]{0:T(128)} %refs_3_.1, s32[8]{0:T(128)} %refs_4_.1, s32[1]{0:T(128)S(6)} %copy.11.refs_5_, bf16[256,1024]{1,0:T(8,128)(2,1)} %refs_6_.1, ...), custom_call_target="tpu_custom_call" | custom-call | tf_op jit(solution)/shard_map/pallas_call | solution.py:352
  40.4 1.1 %shard_map.101 = bf16[256,4,256]{2,1,0:T(4,128)(2,1)} custom-call(bf16[4,256,256]{2,1,0:T(8,128)(2,1)S(1)} %shard_map.100.stacked), custom_call_target="tpu_custom_call" | custom-call | tf_op jit(solution)/shard_map/pallas_call | solution.py:382

commit v7 on v6

--- a/solution.py
+++ b/solution.py
@@ -30,9 +30,10 @@
     outer = jnp.where(odd == 0, has_left, has_right)
     sibling = (r + 1 - 2 * odd, c)
     far_right, far_left = (lax.rem(r + 2, n_row), c), (lax.rem(r + n_row - 2, n_row), c)
+    across = (r - 1 + 2 * odd, c)
     col_right, col_left = (r, lax.rem(c + 1, n_col)), (r, lax.rem(c + n_col - 1, n_col))
     narrow = range(wide, passes)
-    row_parts = [2 if stage == 1 + wide else 1 for stage in range(1 + passes)]
+    mixed = [stage in (0, wide, 1 + wide) for stage in range(1 + passes)]
     col_across = (r, lax.rem(c + 2, n_col))
     node_rows = blocks * BS
     piece, tall = node_rows // 4, node_rows // 2
@@ -46,6 +47,7 @@
 
     pl.when(has_right)(lambda: greet(far_right))
     pl.when(has_left)(lambda: greet(far_left))
+    pl.when(outer)(lambda: greet(across))
     def along_line(by):
         return (r - lax.rem(r, line) + lax.rem(r + 2 * by, line), c)
 
@@ -72,8 +74,8 @@
     for copy in loads + mask_loads:
         copy.start()
     loads[0].wait()
-    pl.semaphore_wait(
-        barrier, 3 + LINE + has_left.astype(jnp.int32) + has_right.astype(jnp.int32))
+    peers = sum(flag.astype(jnp.int32) for flag in (has_left, has_right, outer))
+    pl.semaphore_wait(barrier, 3 + LINE + peers)
 
     def remote(src, dst, send, recv, device):
         return pltpu.make_async_remote_copy(
@@ -83,8 +85,8 @@
     def row_copy(stage, i, part):
         src, dst, device = (
             (2, 0, far_right), (2, 4, far_left), (2, 1 + 2 * odd, sibling),
-            (4 - 4 * odd, 3 - 2 * odd, sibling))[i]
-        size = blocks // row_parts[stage]
+            (4 - 4 * odd, 3 - 2 * odd, sibling), (2, 3 - 2 * odd, across))[i]
+        size = blocks // 2 if mixed[stage] else blocks
         pairs = [ext[stage].at[pl.ds(n * blocks + part * size, size)] for n in (src, dst)]
         recv = far_recv.at[stage, part] if i < 2 else near_recv.at[stage]
         return remote(*pairs, row_send.at[stage], recv, device)
@@ -92,7 +94,13 @@
     def row_start(stage, part):
         pl.when(has_right)(lambda: row_copy(stage, 0, part).start())
         pl.when(has_left)(lambda: row_copy(stage, 1, part).start())
+        if part:
+            pl.when(outer)(lambda: row_copy(stage, 4, part).start())
         row_copy(stage, 2, part).start()
+
+    def row_start_all(stage):
+        for part in range(1 + mixed[stage]):
+            row_start(stage, part)
 
     def one_of(flag, stage, many, few, sem):
         pl.when(flag)(lambda: wait_for(ext[stage].at[pl.ds(0, many)], sem))
@@ -101,19 +109,24 @@
     both = jnp.logical_and(has_left, has_right)
 
     def row_wait(stage):
-        size = blocks // row_parts[stage]
-        for part in range(row_parts[stage]):
-            one_of(both, stage, 2 * size, size, far_recv.at[stage, part])
-            pl.when(inner)(lambda: row_copy(stage, 3, part).start())
+        size = blocks // 2 if mixed[stage] else blocks
+        one_of(both, stage, 2 * size, size, far_recv.at[stage, 0])
+        pl.when(inner)(lambda: row_copy(stage, 3, 0).start())
+        if mixed[stage]:
+            one_of(both, stage, 2 * size, size, far_recv.at[stage, 1])
         one_of(outer, stage, 2 * blocks, blocks, near_recv.at[stage])
 
     def row_drain(stage):
         sent = row_send.at[stage]
-        pl.when(both)(lambda: wait_for(ext[stage].at[pl.ds(0, 4 * blocks)], sent))
+        half = blocks // 2
+        if mixed[stage]:
+            one_of(both, stage, 8 * half, 5 * half, sent)
+            return
+        pl.when(both)(lambda: wait_for(ext[stage].at[pl.ds(0, 8 * half)], sent))
 
         @pl.when(jnp.logical_not(both))
         def _():
-            one_of(inner, stage, 3 * blocks, 2 * blocks, sent)
+            one_of(inner, stage, 6 * half, 4 * half, sent)
 
     def rows(j):
         return pl.ds(j * piece, piece)
@@ -182,7 +195,7 @@
         blocks_held = spread_w.at[odd]
         return remote(blocks_held, blocks_held, w_send.at[2], w_recv.at[2], sibling)
 
-    row_start(0, 0)
+    row_start_all(0)
     wait_for(w2, load_sem.at[7])
     for k in (2, 1, 3):
         weight_copy(k).start()
@@ -276,7 +289,7 @@
     for p in narrow[1:]:
         for part in (0, 1):
             send_dropped(p, part)
-        row_start(1 + p, 0)
+        row_start_all(1 + p)
     share_forward(wide)
     share_forward(1)
     wait_for(spread_w.at[odd, :, pl.ds(0, 3 * piece)], w_recv.at[1])
@@ -298,7 +311,7 @@
         value = project(1).astype(BF16)
         for b in range(blocks):
             ext[1 + p][2 * blocks + b] = value[b * BS:(b + 1) * BS]
-        row_start(1 + p, 0)
+        row_start_all(1 + p)
         self_wide[p] = project(0)
 
     for i, p in enumerate(narrow):

time: 41.6 us -> 41 us (0.986)
  Pallas kernels: 40.8 us -> 40.2 us
    pallas_call x1, Pallas kernels: 39.7 us -> 39.2 us  [on_device(): pl.pallas_call(functools.partial(fused, n_row, n_col, passes, wide, block...]
where the time goes in v7:
time: 41 us; the launch traced here: 40.9 us
  Pallas kernels  40.2 us (98%)
  between operations  0.66 us (2%)
    pallas_call x1, Pallas kernels, on_device(): pl.pallas_call(functools.partial(fused, n_row, n_col, passes, wide, block...  39.2 us
    pallas_call x1, Pallas kernels, on_device(): pl.pallas_call(interleave, out_shape=jax.ShapeDtypeStruct((node_rows, pas...  1.07 us

profile of v7, /device:TPU:103, one launch (start us, length us, event | category | flops | bytes accessed | tf_op | source)
XLA Modules:
  0.0 40.9 jit_solution(6832831990926719403)
XLA Ops:
  0.7 39.2 %shard_map.100.stacked = bf16[4,256,256]{2,1,0:T(8,128)(2,1)S(1)} custom-call(bf16[2,128,256]{2,1,0:T(8,128)(2,1)} %bitcast.1, s32[256,4,256]{2,1,0:T(4,128)} %refs_1_.1, bf16[8,128,128]{2,1,0:T(8,128)(2,1)} %refs_2_.1, s32[8]{0:T(128)} %refs_3_.1, s32[8]{0:T(128)} %refs_4_.1, s32[1]{0:T(128)S(6)} %copy.11.refs_5_, bf16[256,1024]{1,0:T(8,128)(2,1)} %refs_6_.1, ...), custom_call_target="tpu_custom_call" | custom-call | tf_op jit(solution)/shard_map/pallas_call | solution.py:365
  39.8 1.1 %shard_map.101 = bf16[256,4,256]{2,1,0:T(4,128)(2,1)} custom-call(bf16[4,256,256]{2,1,0:T(8,128)(2,1)S(1)} %shard_map.100.stacked), custom_call_target="tpu_custom_call" | custom-call | tf_op jit(solution)/shard_map/pallas_call | solution.py:395

commit v8 on v7

--- a/solution.py
+++ b/solution.py
@@ -9,6 +9,7 @@
 
 BS = 128
 LINE = 4
+CHUNKS = 4
 MESH = pl.DeviceIdType.MESH
 BF16, F32 = jnp.bfloat16, jnp.float32
 
@@ -20,8 +21,8 @@
     rows_s, cols_s, count_s, adj_v, placed, scale, ws1, wn1, w2, mask_v = rest[:10]
     self_term, term, mid, relayed, got, spread_w, shared, self_wide = rest[10:18]
     ext = rest[18:19 + passes]
-    (load_sem, row_send, far_recv, near_recv, col_send, col_recv, share_send, share_recv,
-     w_send, w_recv) = rest[19 + passes:]
+    (load_sem, row_send, far_recv, near_recv, sent, col_recv, share_recv,
+     w_recv) = rest[19 + passes:]
 
     r, c = lax.axis_index("row"), lax.axis_index("col")
     odd = lax.rem(r, 2)
@@ -38,7 +39,8 @@
     node_rows = blocks * BS
     piece, tall = node_rows // 4, node_rows // 2
     line = 2 * LINE
-    spot = lax.rem(r // 2, LINE)
+    spot, upper = lax.rem(r // 2, LINE), lax.rem(r // (2 * LINE), 2)
+    paired = (r + line * (1 - 2 * upper), c)
 
     barrier = pltpu.get_barrier_semaphore()
 
@@ -51,20 +53,20 @@
     def along_line(by):
         return (r - lax.rem(r, line) + lax.rem(r + 2 * by, line), c)
 
-    for device in (sibling, col_right, col_left, col_across) + tuple(
+    for device in (sibling, col_right, col_left, col_across, paired) + tuple(
             along_line(by) for by in range(1, LINE)):
         greet(device)
 
     loads = []
     own = ext[0].at[pl.ds(2 * blocks, blocks)]
     for i, src, dst in (
-        (0, features, own), (1, adj, adj_v), (2, adj_rows, rows_s), (3, adj_cols, cols_s),
-        (4, adj_count, count_s), (5, w_self_one, ws1), (6, w_neigh_one, wn1),
-        (7, w_self_two, w2.at[0]), (7, w_neigh_two, w2.at[1]),
+        (0, features, own), (5, adj, adj_v), (2, adj_rows, rows_s), (3, adj_cols, cols_s),
+        (4, adj_count, count_s), (5, w_self_one, ws1), (5, w_neigh_one, wn1),
+        (6, w_self_two, w2.at[0]), (6, w_neigh_two, w2.at[1]),
     ):
         loads.append(pltpu.make_async_copy(src, dst, load_sem.at[i]))
     mask_loads = [
-        pltpu.make_async_copy(masks.at[:, p, :], mask_v.at[p], load_sem.at[8])
+        pltpu.make_async_copy(masks.at[:, p, :], mask_v.at[p], load_sem.at[7])
         for p in range(passes)
     ]
 
@@ -75,7 +77,7 @@
         copy.start()
     loads[0].wait()
     peers = sum(flag.astype(jnp.int32) for flag in (has_left, has_right, outer))
-    pl.semaphore_wait(barrier, 3 + LINE + peers)
+    pl.semaphore_wait(barrier, 4 + LINE + peers)
 
     def remote(src, dst, send, recv, device):
         return pltpu.make_async_remote_copy(
@@ -89,7 +91,7 @@
         size = blocks // 2 if mixed[stage] else blocks
         pairs = [ext[stage].at[pl.ds(n * blocks + part * size, size)] for n in (src, dst)]
         recv = far_recv.at[stage, part] if i < 2 else near_recv.at[stage]
-        return remote(*pairs, row_send.at[stage], recv, device)
+        return remote(*pairs, row_send.at[0 if mixed[stage] else 1], recv, device)
 
     def row_start(stage, part):
         pl.when(has_right)(lambda: row_copy(stage, 0, part).start())
@@ -116,17 +118,25 @@
             one_of(both, stage, 2 * size, size, far_recv.at[stage, 1])
         one_of(outer, stage, 2 * blocks, blocks, near_recv.at[stage])
 
-    def row_drain(stage):
-        sent = row_send.at[stage]
-        half = blocks // 2
-        if mixed[stage]:
-            one_of(both, stage, 8 * half, 5 * half, sent)
-            return
-        pl.when(both)(lambda: wait_for(ext[stage].at[pl.ds(0, 8 * half)], sent))
+    def row_drain():
+        def drained(stages, blocks_each, sem):
+            wait_for(self_term.at[pl.ds(0, stages), pl.ds(0, blocks_each), pl.ds(0, BS // 2)],
+                     sem)
+
+        some = sum(mixed)
+        others = len(mixed) - some
+
+        @pl.when(both)
+        def _():
+            whole = self_term.at[pl.ds(0, some), :, pl.ds(0, BS)]
+            wait_for(whole, row_send.at[0])
+            drained(2 * others, 4, row_send.at[1])
 
         @pl.when(jnp.logical_not(both))
         def _():
-            one_of(inner, stage, 6 * half, 4 * half, sent)
+            drained(5, some, row_send.at[0])
+            pl.when(inner)(lambda: drained(others + 1, 4, row_send.at[1]))
+            pl.when(jnp.logical_not(inner))(lambda: drained(others, 4, row_send.at[1]))
 
     def rows(j):
         return pl.ds(j * piece, piece)
@@ -148,7 +158,7 @@
             k = 4 - onward(j)
             src, dst, device = t.at[k, rows(j)], g.at[1 - j % 2, rows(j)], toward(j + 1)
         recv = col_recv.at[stage, 0 if i < 4 else 1, j // 2]
-        return remote(src, dst, col_send.at[stage], recv, device)
+        return remote(src, dst, sent, recv, device)
 
     def share_copy(stage, i):
         held = shared.at[stage]
@@ -159,7 +169,7 @@
             src, dst, device = 0, 4 - onward(j), toward(j + 1)
         else:
             src, dst, device = onward(j), 2, toward(j)
-        return remote(held.at[src, rows(j)], held.at[dst, rows(j)], share_send.at[stage],
+        return remote(held.at[src, rows(j)], held.at[dst, rows(j)], sent,
                       share_recv.at[stage, j // 2 if i < 4 else 2], device)
 
     def share_start(stage, *which):
@@ -182,29 +192,37 @@
 
     part_rows = pl.ds(pl.multiple_of(spot * piece, piece), piece)
 
+    slim = piece // 2
+    slim_rows = pl.ds(pl.multiple_of(spot * piece + upper * slim, slim), slim)
+
     def weight_copy(k):
         device = {1: col_right, 2: col_across, 3: col_left}[k]
-        return remote(w2.at[odd, part_rows, quarter(k)], spread_w.at[odd, k - 1, part_rows],
-                      w_send.at[0], w_recv.at[0], device)
+        return remote(w2.at[odd, slim_rows, quarter(k)], spread_w.at[odd, k - 1, slim_rows],
+                      sent, w_recv.at[0], device)
+
+    def pair_copy():
+        part = spread_w.at[odd, :, slim_rows]
+        return remote(part, part, sent, w_recv.at[3], paired)
 
     def line_copy(by):
         part = spread_w.at[odd, :, part_rows]
-        return remote(part, part, w_send.at[1], w_recv.at[1], along_line(by))
+        return remote(part, part, sent, w_recv.at[1], along_line(by))
 
     def weight_forward():
         blocks_held = spread_w.at[odd]
-        return remote(blocks_held, blocks_held, w_send.at[2], w_recv.at[2], sibling)
+        return remote(blocks_held, blocks_held, sent, w_recv.at[2], sibling)
 
     row_start_all(0)
-    wait_for(w2, load_sem.at[7])
+    wait_for(w2, load_sem.at[6])
     for k in (2, 1, 3):
         weight_copy(k).start()
-    wait_for(mask_v, load_sem.at[8])
+    wait_for(mask_v, load_sem.at[7])
     for p in range(wide):
         shared[p, 0] = (2 * mask_v[p]).astype(BF16)
     share_start(0, 0, 1, 2, 3, 4, 5, 6, 7)
-    share_start(1, 0, 1, 2, 3)
-    for copy in loads[1:5]:
+    share_start(1, 0, 1, 2, 3, 4, 5, 6, 7)
+    wait_for(self_term.at[:, 0], load_sem.at[5])
+    for copy in loads[2:5]:
         copy.wait()
     me = r * blocks - 2 * blocks
     local = [jnp.clip(cols_s[s] - me, 0, 5 * blocks - 1) for s in range(slots)]
@@ -262,16 +280,15 @@
         return (term[stage, 0, here].astype(F32) + got[stage, 0, here].astype(F32)
                 + got[stage, 1, here].astype(F32))
 
-    loads[5].wait()
     self_project(0, ws1)
-    loads[6].wait()
+    wait_for(spread_w.at[odd, :, slim_rows], w_recv.at[0])
+    pair_copy().start()
     spread_terms(0, 0, wn1)
-    wait_for(spread_w.at[odd, :, part_rows], w_recv.at[0])
+    wait_for(spread_w.at[odd, :, slim_rows], w_recv.at[3])
     for by in (2, 1, 3):
         line_copy(by).start()
     for part in (0, 1):
         relay(0, part)
-    share_start(1, 4, 5, 6, 7)
     share_forward(0)
 
     def send_dropped(p, part):
@@ -329,23 +346,23 @@
     for i, p in enumerate(narrow):
         for part in (0, 1):
             out[p, tall_rows(part)] = gathered(1 + i, part).astype(BF16)
-    for stage in range(1 + passes):
-        row_drain(stage)
-    for stage in range(1 + len(narrow)):
-        wait_for(term.at[stage, pl.ds(0, 3)], col_send.at[stage])
-    for stage in range(1 + wide):
-        wait_for(shared.at[stage, pl.ds(0, 3)], share_send.at[stage])
-    wait_for(spread_w.at[odd, :, part_rows], w_send.at[0])
-    wait_for(spread_w.at[odd, :, pl.ds(0, 3 * piece)], w_send.at[1])
-    wait_for(spread_w.at[odd], w_send.at[2])
-
-
-def interleave(stacked, out):
-    passes, rows, _ = stacked.shape
-    step = 32
-    for low in range(0, rows, step):
-        part = stacked[:, low:low + step, :].astype(F32)
-        out[low:low + step] = jnp.swapaxes(part, 0, 1).astype(BF16)
+    row_drain()
+    wait_for(self_term.at[pl.ds(0, 3)], sent)
+
+
+def interleave(stacked, out, held, sem):
+    rows = stacked.shape[1]
+    step, size = rows // 8, rows // CHUNKS
+    copies = []
+    for chunk in range(CHUNKS):
+        for low in range(chunk * size, (chunk + 1) * size, step):
+            part = stacked[:, low:low + step, :].astype(F32)
+            held[low:low + step] = jnp.swapaxes(part, 0, 1).astype(BF16)
+        span = pl.ds(chunk * size, size)
+        copies.append(pltpu.make_async_copy(held.at[span], out.at[span], sem.at[chunk]))
+        copies[-1].start()
+    for copy in copies:
+        copy.wait()
 
 
 def solution(mesh):
@@ -384,9 +401,8 @@
                 pltpu.VMEM((1 + wide, n_col) + tile, BF16),
                 pltpu.VMEM((wide,) + tile, F32),
             ] + [ext] * (1 + passes) + [
-                dma((9,)), dma((1 + passes,)), dma((1 + passes, 2)), dma((1 + passes,)),
-                dma((scatters,)), dma((scatters, 2, 2)), dma((1 + wide,)),
-                dma((1 + wide, 3)), dma((3,)), dma((3,)),
+                dma((8,)), dma((2,)), dma((1 + passes, 2)), dma((1 + passes,)), dma(()),
+                dma((scatters, 2, 2)), dma((1 + wide, 3)), dma((4,)),
             ],
             compiler_params=pltpu.CompilerParams(
                 collective_id=0, has_side_effects=True, vmem_limit_bytes=48 * 2**20),
@@ -396,7 +412,8 @@
             interleave,
             out_shape=jax.ShapeDtypeStruct((node_rows, passes, width), BF16),
             in_specs=[vmem_spec],
-            out_specs=vmem_spec,
+            out_specs=any_spec,
+            scratch_shapes=[pltpu.VMEM((node_rows, passes, width), BF16), dma((CHUNKS,))],
             compiler_params=pltpu.CompilerParams(vmem_limit_bytes=16 * 2**20),
         )(stacked)
 

time: 41 us -> 40.4 us (0.985)
  Pallas kernels: 40.2 us -> 39.6 us
    pallas_call x1, Pallas kernels: 39.2 us -> 38.6 us  [on_device(): pl.pallas_call(functools.partial(fused, n_row, n_col, passes, wide, block...]
where the time goes in v8:
time: 40.4 us; the launch traced here: 40.3 us
  Pallas kernels  39.6 us (98%)
  between operations  0.66 us (2%)
    pallas_call x1, Pallas kernels, on_device(): pl.pallas_call(functools.partial(fused, n_row, n_col, passes, wide, block...  38.6 us
    pallas_call x1, Pallas kernels, on_device(): pl.pallas_call(interleave, out_shape=jax.ShapeDtypeStruct((node_rows, pas...  0.97 us

profile of v8, /device:TPU:103, one launch (start us, length us, event | category | flops | bytes accessed | tf_op | source)
XLA Modules:
  0.0 40.3 jit_solution(6808627838424182945)
XLA Ops:
  0.7 38.6 %shard_map.100.stacked = bf16[4,256,256]{2,1,0:T(8,128)(2,1)S(1)} custom-call(bf16[2,128,256]{2,1,0:T(8,128)(2,1)} %bitcast.1, s32[256,4,256]{2,1,0:T(4,128)} %refs_1_.1, bf16[8,128,128]{2,1,0:T(8,128)(2,1)} %refs_2_.1, s32[8]{0:T(128)} %refs_3_.1, s32[8]{0:T(128)} %refs_4_.1, s32[1]{0:T(128)S(6)} %copy.11.refs_5_, bf16[256,1024]{1,0:T(8,128)(2,1)} %refs_6_.1, ...), custom_call_target="tpu_custom_call" | custom-call | tf_op jit(solution)/shard_map/pallas_call | solution.py:382
  39.3 1.0 %shard_map.101 = bf16[256,4,256]{2,1,0:T(4,128)(2,1)} custom-call(bf16[4,256,256]{2,1,0:T(8,128)(2,1)S(1)} %shard_map.100.stacked), custom_call_target="tpu_custom_call" | custom-call | tf_op jit(solution)/shard_map/pallas_call | solution.py:411

commit v9 on v8

--- a/solution.py
+++ b/solution.py
@@ -34,6 +34,7 @@
     across = (r - 1 + 2 * odd, c)
     col_right, col_left = (r, lax.rem(c + 1, n_col)), (r, lax.rem(c + n_col - 1, n_col))
     narrow = range(wide, passes)
+    scatters = 1 + len(narrow)
     mixed = [stage in (0, wide, 1 + wide) for stage in range(1 + passes)]
     col_across = (r, lax.rem(c + 2, n_col))
     node_rows = blocks * BS
@@ -60,13 +61,13 @@
     loads = []
     own = ext[0].at[pl.ds(2 * blocks, blocks)]
     for i, src, dst in (
-        (0, features, own), (5, adj, adj_v), (2, adj_rows, rows_s), (3, adj_cols, cols_s),
-        (4, adj_count, count_s), (5, w_self_one, ws1), (5, w_neigh_one, wn1),
-        (6, w_self_two, w2.at[0]), (6, w_neigh_two, w2.at[1]),
+        (0, features, own), (4, adj, adj_v), (1, adj_rows, rows_s), (2, adj_cols, cols_s),
+        (3, adj_count, count_s), (4, w_self_one, ws1), (4, w_neigh_one, wn1),
+        (5, w_self_two, w2.at[0]), (5, w_neigh_two, w2.at[1]),
     ):
         loads.append(pltpu.make_async_copy(src, dst, load_sem.at[i]))
     mask_loads = [
-        pltpu.make_async_copy(masks.at[:, p, :], mask_v.at[p], load_sem.at[7])
+        pltpu.make_async_copy(masks.at[:, p, :], mask_v.at[p], load_sem.at[6])
         for p in range(passes)
     ]
 
@@ -90,7 +91,7 @@
             (4 - 4 * odd, 3 - 2 * odd, sibling), (2, 3 - 2 * odd, across))[i]
         size = blocks // 2 if mixed[stage] else blocks
         pairs = [ext[stage].at[pl.ds(n * blocks + part * size, size)] for n in (src, dst)]
-        recv = far_recv.at[stage, part] if i < 2 else near_recv.at[stage]
+        recv = far_recv.at[stage] if i < 2 and not part else near_recv.at[stage]
         return remote(*pairs, row_send.at[0 if mixed[stage] else 1], recv, device)
 
     def row_start(stage, part):
@@ -112,11 +113,16 @@
 
     def row_wait(stage):
         size = blocks // 2 if mixed[stage] else blocks
-        one_of(both, stage, 2 * size, size, far_recv.at[stage, 0])
+        one_of(both, stage, 2 * size, size, far_recv.at[stage])
         pl.when(inner)(lambda: row_copy(stage, 3, 0).start())
-        if mixed[stage]:
-            one_of(both, stage, 2 * size, size, far_recv.at[stage, 1])
-        one_of(outer, stage, 2 * blocks, blocks, near_recv.at[stage])
+        if not mixed[stage]:
+            one_of(outer, stage, 2 * blocks, blocks, near_recv.at[stage])
+            return
+        pl.when(both)(lambda: wait_for(ext[stage].at[pl.ds(0, 6 * size)], near_recv.at[stage]))
+
+        @pl.when(jnp.logical_not(both))
+        def _():
+            one_of(outer, stage, 5 * size, 3 * size, near_recv.at[stage])
 
     def row_drain():
         def drained(stages, blocks_each, sem):
@@ -146,6 +152,12 @@
 
     def onward(j):
         return (1, 3)[j % 2]
+
+    def first_recv(stage, part):
+        return col_recv.at[3 * stage + part]
+
+    def last_recv(stage, part):
+        return col_recv.at[3 * stage + 2 if stage or not part else 3 * scatters]
 
     def col_copy(stage, i):
         t, g = term.at[stage], got.at[stage]
@@ -157,8 +169,13 @@
         else:
             k = 4 - onward(j)
             src, dst, device = t.at[k, rows(j)], g.at[1 - j % 2, rows(j)], toward(j + 1)
-        recv = col_recv.at[stage, 0 if i < 4 else 1, j // 2]
+        recv = first_recv(stage, j // 2) if i < 4 else last_recv(stage, j // 2)
         return remote(src, dst, sent, recv, device)
+
+    def shared_recv(stage, n):
+        if stage < wide:
+            return share_recv.at[2 * stage + n // 2]
+        return share_recv.at[2 * wide + n]
 
     def share_copy(stage, i):
         held = shared.at[stage]
@@ -170,7 +187,7 @@
         else:
             src, dst, device = onward(j), 2, toward(j)
         return remote(held.at[src, rows(j)], held.at[dst, rows(j)], sent,
-                      share_recv.at[stage, j // 2 if i < 4 else 2], device)
+                      shared_recv(stage, j // 2 if i < 4 else 2), device)
 
     def share_start(stage, *which):
         for i in which:
@@ -180,12 +197,16 @@
         return pl.ds(part * tall, tall)
 
     def share_forward(stage):
+        if stage < wide:
+            wait_for(shared.at[stage, 1], shared_recv(stage, 0))
+            share_start(stage, 8, 9, 10, 11)
+            return
         for part in (0, 1):
-            wait_for(shared.at[stage, 1, tall_rows(part)], share_recv.at[stage, part])
+            wait_for(shared.at[stage, 1, tall_rows(part)], shared_recv(stage, part))
             share_start(stage, 8 + 2 * part, 9 + 2 * part)
 
     def share_wait(stage):
-        wait_for(shared.at[stage, pl.ds(1, 2)], share_recv.at[stage, 2])
+        wait_for(shared.at[stage, pl.ds(1, 2)], shared_recv(stage, 2))
 
     def quarter(k):
         return pl.ds(pl.multiple_of(lax.rem(c + k, n_col) * node_rows, node_rows), node_rows)
@@ -213,15 +234,15 @@
         return remote(blocks_held, blocks_held, sent, w_recv.at[2], sibling)
 
     row_start_all(0)
-    wait_for(w2, load_sem.at[6])
+    wait_for(w2, load_sem.at[5])
     for k in (2, 1, 3):
         weight_copy(k).start()
-    wait_for(mask_v, load_sem.at[7])
+    wait_for(mask_v, load_sem.at[6])
     for p in range(wide):
         shared[p, 0] = (2 * mask_v[p]).astype(BF16)
     share_start(0, 0, 1, 2, 3, 4, 5, 6, 7)
     share_start(1, 0, 1, 2, 3, 4, 5, 6, 7)
-    wait_for(self_term.at[:, 0], load_sem.at[5])
+    wait_for(self_term.at[:, 0], load_sem.at[4])
     for copy in loads[2:5]:
         copy.wait()
     me = r * blocks - 2 * blocks
@@ -267,7 +288,7 @@
         spread(col_stage, lambda k: self_term[row_stage, k] + product(agg, w_neigh, k))
 
     def relay(stage, part):
-        wait_for(mid.at[stage, tall_rows(part)], col_recv.at[stage, 0, part])
+        wait_for(mid.at[stage, tall_rows(part)], first_recv(stage, part))
         for j in (2 * part, 2 * part + 1):
             both_terms = (term[stage, onward(j), rows(j)].astype(F32)
                           + mid[stage, rows(j)].astype(F32))
@@ -275,7 +296,10 @@
             col_copy(stage, 4 + j).start()
 
     def gathered(stage, part):
-        wait_for(got.at[stage, :, tall_rows(part)], col_recv.at[stage, 1, part])
+        if stage == 0:
+            wait_for(got.at[stage, :, tall_rows(part)], last_recv(stage, part))
+        elif part == 0:
+            wait_for(got.at[stage], last_recv(stage, part))
         here = tall_rows(part)
         return (term[stage, 0, here].astype(F32) + got[stage, 0, here].astype(F32)
                 + got[stage, 1, here].astype(F32))
@@ -401,8 +425,8 @@
                 pltpu.VMEM((1 + wide, n_col) + tile, BF16),
                 pltpu.VMEM((wide,) + tile, F32),
             ] + [ext] * (1 + passes) + [
-                dma((8,)), dma((2,)), dma((1 + passes, 2)), dma((1 + passes,)), dma(()),
-                dma((scatters, 2, 2)), dma((1 + wide, 3)), dma((4,)),
+                dma((7,)), dma((2,)), dma((1 + passes,)), dma((1 + passes,)), dma(()),
+                dma((3 * scatters + 1,)), dma((2 * wide + 3,)), dma((4,)),
             ],
             compiler_params=pltpu.CompilerParams(
                 collective_id=0, has_side_effects=True, vmem_limit_bytes=48 * 2**20),

time: 40.4 us -> 40.3 us (level)
  no operation moved by 1% of the time
where the time goes in v9:
time: 40.3 us; the launch traced here: 40.2 us
  Pallas kernels  39.5 us (98%)
  between operations  0.66 us (2%)
    pallas_call x1, Pallas kernels, on_device(): pl.pallas_call(functools.partial(fused, n_row, n_col, passes, wide, block...  38.5 us
    pallas_call x1, Pallas kernels, on_device(): pl.pallas_call(interleave, out_shape=jax.ShapeDtypeStruct((node_rows, pas...  0.97 us

profile of v9, /device:TPU:103, one launch (start us, length us, event | category | flops | bytes accessed | tf_op | source)
XLA Modules:
  0.0 40.2 jit_solution(2664801196431538759)
XLA Ops:
  0.7 38.5 %shard_map.100.stacked = bf16[4,256,256]{2,1,0:T(8,128)(2,1)S(1)} custom-call(bf16[2,128,256]{2,1,0:T(8,128)(2,1)} %bitcast.1, s32[256,4,256]{2,1,0:T(4,128)} %refs_1_.1, bf16[8,128,128]{2,1,0:T(8,128)(2,1)} %refs_2_.1, s32[8]{0:T(128)} %refs_3_.1, s32[8]{0:T(128)} %refs_4_.1, s32[1]{0:T(128)S(6)} %copy.11.refs_5_, bf16[256,1024]{1,0:T(8,128)(2,1)} %refs_6_.1, ...), custom_call_target="tpu_custom_call" | custom-call | tf_op jit(solution)/shard_map/pallas_call | solution.py:406
  39.2 1.0 %shard_map.101 = bf16[256,4,256]{2,1,0:T(4,128)(2,1)} custom-call(bf16[4,256,256]{2,1,0:T(8,128)(2,1)S(1)} %shard_map.100.stacked), custom_call_target="tpu_custom_call" | custom-call | tf_op jit(solution)/shard_map/pallas_call | solution.py:435

commit v10 on v9

--- a/solution.py
+++ b/solution.py
@@ -48,13 +48,15 @@
     def greet(device):
         pl.semaphore_signal(barrier, 1, device_id=device, device_id_type=MESH)
 
+    for device in (col_right, col_left, col_across):
+        greet(device)
     pl.when(has_right)(lambda: greet(far_right))
     pl.when(has_left)(lambda: greet(far_left))
     pl.when(outer)(lambda: greet(across))
     def along_line(by):
         return (r - lax.rem(r, line) + lax.rem(r + 2 * by, line), c)
 
-    for device in (sibling, col_right, col_left, col_across, paired) + tuple(
+    for device in (sibling, paired) + tuple(
             along_line(by) for by in range(1, LINE)):
         greet(device)
 
@@ -74,7 +76,7 @@
     def wait_for(ref, sem):
         pltpu.make_async_copy(ref, ref, sem).wait()
 
-    for copy in loads + mask_loads:
+    for copy in loads[:1] + loads[7:] + mask_loads + loads[1:7]:
         copy.start()
     loads[0].wait()
     peers = sum(flag.astype(jnp.int32) for flag in (has_left, has_right, outer))

time: 40.3 us -> 40.3 us (level)
  no operation moved by 1% of the time
where the time goes in v10:
time: 40.3 us; the launch traced here: 40.2 us
  Pallas kernels  39.5 us (98%)
  between operations  0.66 us (2%)
    pallas_call x1, Pallas kernels, on_device(): pl.pallas_call(functools.partial(fused, n_row, n_col, passes, wide, block...  38.5 us
    pallas_call x1, Pallas kernels, on_device(): pl.pallas_call(interleave, out_shape=jax.ShapeDtypeStruct((node_rows, pas...  0.97 us

profile of v10, /device:TPU:103, one launch (start us, length us, event | category | flops | bytes accessed | tf_op | source)
XLA Modules:
  0.0 40.2 jit_solution(11468380303915673848)
XLA Ops:
  0.7 38.5 %shard_map.100.stacked = bf16[4,256,256]{2,1,0:T(8,128)(2,1)S(1)} custom-call(bf16[2,128,256]{2,1,0:T(8,128)(2,1)} %bitcast.1, s32[256,4,256]{2,1,0:T(4,128)} %refs_1_.1, bf16[8,128,128]{2,1,0:T(8,128)(2,1)} %refs_2_.1, s32[8]{0:T(128)} %refs_3_.1, s32[8]{0:T(128)} %refs_4_.1, s32[1]{0:T(128)S(6)} %copy.11.refs_5_, bf16[256,1024]{1,0:T(8,128)(2,1)} %refs_6_.1, ...), custom_call_target="tpu_custom_call" | custom-call | tf_op jit(solution)/shard_map/pallas_call | solution.py:408
  39.2 1.0 %shard_map.101 = bf16[256,4,256]{2,1,0:T(4,128)(2,1)} custom-call(bf16[4,256,256]{2,1,0:T(8,128)(2,1)S(1)} %shard_map.100.stacked), custom_call_target="tpu_custom_call" | custom-call | tf_op jit(solution)/shard_map/pallas_call | solution.py:437

commit v11 on v9

--- a/solution.py
+++ b/solution.py
@@ -9,7 +9,7 @@
 
 BS = 128
 LINE = 4
-CHUNKS = 4
+CHUNKS = 8
 MESH = pl.DeviceIdType.MESH
 BF16, F32 = jnp.bfloat16, jnp.float32
 

time: 40.3 us -> 40.3 us (level)
  no operation moved by 1% of the time
where the time goes in v11:
time: 40.3 us; the launch traced here: 40.2 us
  Pallas kernels  39.5 us (98%)
  between operations  0.66 us (2%)
    pallas_call x1, Pallas kernels, on_device(): pl.pallas_call(functools.partial(fused, n_row, n_col, passes, wide, block...  38.5 us
    pallas_call x1, Pallas kernels, on_device(): pl.pallas_call(interleave, out_shape=jax.ShapeDtypeStruct((node_rows, pas...  0.98 us

profile of v11, /device:TPU:103, one launch (start us, length us, event | category | flops | bytes accessed | tf_op | source)
XLA Modules:
  0.0 40.2 jit_solution(5287583473882557673)
XLA Ops:
  0.7 38.5 %shard_map.100.stacked = bf16[4,256,256]{2,1,0:T(8,128)(2,1)S(1)} custom-call(bf16[2,128,256]{2,1,0:T(8,128)(2,1)} %bitcast.1, s32[256,4,256]{2,1,0:T(4,128)} %refs_1_.1, bf16[8,128,128]{2,1,0:T(8,128)(2,1)} %refs_2_.1, s32[8]{0:T(128)} %refs_3_.1, s32[8]{0:T(128)} %refs_4_.1, s32[1]{0:T(128)S(6)} %copy.11.refs_5_, bf16[256,1024]{1,0:T(8,128)(2,1)} %refs_6_.1, ...), custom_call_target="tpu_custom_call" | custom-call | tf_op jit(solution)/shard_map/pallas_call | solution.py:406
  39.2 1.0 %shard_map.101 = bf16[256,4,256]{2,1,0:T(4,128)(2,1)} custom-call(bf16[4,256,256]{2,1,0:T(8,128)(2,1)S(1)} %shard_map.100.stacked), custom_call_target="tpu_custom_call" | custom-call | tf_op jit(solution)/shard_map/pallas_call | solution.py:435
